TPU v7x, 32 devices: a whole 2x2x4 slice. The times are simulated.
32 devices in a mesh: dp: 16 (over z, y, core), tensor: 2 (over x).
Axes of the slice: x: 2, y: 2, z: 4, core: 2. Of those that a mesh axis runs over, the one named last changes fastest.
Arguments:
- tokens: bfloat16 [16, 1024, 1024], P('dp', 'tensor'), may hold values from -6 to 6
- segment_ids: int32 [16, 1024], P('dp'), may hold values from 0 to 2, as said below
- norm_gains: float32 [2, 1024], replicated, may hold values from 0.25 to 1.75
- w_mixer_in: bfloat16 [1024, 4, 8, 128], P('dp', None, 'tensor'), may hold values from -0.1875 to 0.1875
- w_rates: bfloat16 [1024, 2, 8], P('dp', None, 'tensor'), may hold values from -0.1875 to 0.1875
- conv_weight: bfloat16 [3, 4, 8, 128], P(None, None, 'tensor', 'dp'), may hold values from -3 to 3
- a_log: float32 [8], replicated, may hold values from -7 to -3
- out_gain: float32 [128], replicated, may hold values from 0.25 to 1.75
- w_output: bfloat16 [1024, 1024], P('tensor', 'dp'), may hold values from -0.25 to 0.25
- w_gate_up: bfloat16 [1024, 2, 2816], P('dp', None, 'tensor'), may hold values from -0.1875 to 0.1875
- w_down: bfloat16 [2816, 1024], P('tensor', 'dp'), may hold values from -0.21875 to 0.21875
- cotangent: bfloat16 [16, 1024, 1024], P('dp', 'tensor'), may hold values from -6 to 6
Outputs:
- out_tokens: bfloat16 [16, 1024, 1024], P('dp', 'tensor')
- grad_tokens: bfloat16 [16, 1024, 1024], P('dp', 'tensor')
- grad_norm_gains: float32 [2, 1024], replicated
- grad_w_mixer_in: float32 [1024, 4, 8, 128], P('dp', None, 'tensor')
- grad_w_rates: float32 [1024, 2, 8], P('dp', None, 'tensor')
- grad_conv_weight: float32 [3, 4, 8, 128], P(None, None, 'tensor', 'dp')
- grad_a_log: float32 [8], replicated
- grad_out_gain: float32 [128], replicated
- grad_w_output: float32 [1024, 1024], P('tensor', 'dp')
- grad_w_gate_up: float32 [1024, 2, 2816], P('dp', None, 'tensor')
- grad_w_down: float32 [2816, 1024], P('tensor', 'dp')
Inputs may be any that keep to these rules, and one draw needn't show every extreme that they name: `segment_ids`: each sequence holds exactly three documents, numbered 0, 1 and 2 in order along it, each of 200 tokens or more; document numbers never fall along a sequence.
All inputs are finite; a program needn't handle non-finite values.
Results may differ from a plain program's by a relative error of at most 0.022.
Values may be sent and summed in bfloat16 or wider, within the bound.
No kernel may reach another device: no remote copies, remote signals or barrier semaphores. Data moves between devices by JAX's collectives and lax.ppermute only.
A program may use at most 256 MiB of HBM per device.

v0:
```python
import functools

import jax
import jax.numpy as jnp
from jax import lax
from jax.experimental import pallas as pl
from jax.experimental.pallas import tpu as pltpu
from jax.sharding import PartitionSpec as P

CHUNK = 128
WIDTH = 128
HALO = 8
COLUMN_TILE = 256
norm_eps = 1e-05
unit_eps = 1e-06
f32 = jnp.float32
bf16 = jnp.bfloat16

NN = ((1,), (0,))
NT = ((1,), (1,))
TN = ((0,), (0,))


def in_hbm(*arrays):
    return [pltpu.with_memory_space_constraint(array, pltpu.HBM) for array in arrays]


def dot(left, right, dims):
    return lax.dot_general(
        left.astype(bf16), right.astype(bf16), (dims, ((), ())), preferred_element_type=f32
    )


def dot_exact(left, right, dims):
    return lax.dot_general(
        left, right, (dims, ((), ())), precision=lax.Precision.HIGHEST, preferred_element_type=f32
    )


def sigmoid(value):
    return 0.5 * jnp.tanh(0.5 * value) + 0.5


def softplus(value):
    return jnp.maximum(value, 0.0) + jnp.log(1.0 + jnp.exp(-jnp.abs(value)))


def shifted(rows, offset):
    return pltpu.roll(rows, offset, 0)[HALO:] if offset else rows[HALO:]


def conv_terms(rows, keeps):
    return [rows[HALO:]] + [
        jnp.where(keeps[offset], shifted(rows, offset), 0.0) for offset in range(1, 4)
    ]


def conv_sum(terms, conv_ref, part, lanes):
    total = None
    for offset in range(4):
        weight = conv_ref[pl.ds(part * 4 + 3 - offset, 1), lanes]
        term = weight * terms[offset]
        total = term if total is None else total + term
    return total


def lane_column(values, lane):
    return jnp.broadcast_to(values[:, lane : lane + 1], values.shape)


def grids():
    row = lax.broadcasted_iota(jnp.int32, (CHUNK, CHUNK), 0)
    col = lax.broadcasted_iota(jnp.int32, (CHUNK, CHUNK), 1)
    return row, col


def level_masks(row, col):
    masks = []
    shift = 0
    while (1 << shift) < CHUNK:
        near = (row >> (shift + 1)) == (col >> (shift + 1))
        apart = (row >> shift) != (col >> shift)
        masks.append(near & apart)
        shift += 1
    return masks


def unit_lower_inverses(lowers, row, col, beside):
    masks = level_masks(row, col)
    beside = list(beside)
    share = -(-len(beside) // (2 * len(masks[1:])))

    def place():
        for work in beside[:share]:
            work()
        del beside[:share]

    identity = jnp.where(row == col, 1.0, 0.0).astype(f32)
    inverses = [identity - jnp.where(masks[0], lower, 0.0) for lower in lowers]
    for mask in masks[1:]:
        blocks = [jnp.where(mask, lower, 0.0).astype(bf16) for lower in lowers]
        low = [inverse.astype(bf16) for inverse in inverses]
        firsts = [dot(inverse, block, NN) for inverse, block in zip(low, blocks)]
        place()
        firsts = [dot(first, inverse, NN) for first, inverse in zip(firsts, low)]
        place()
        inverses = [inverse - first for inverse, first in zip(inverses, firsts)]
    return inverses


def chunk_scales(heads, rates, neg_rate, seg, last_seen, row, col):
    steps = neg_rate * softplus(rates)
    lower_ones = jnp.where(row >= col, 1.0, 0.0).astype(f32)
    cumulative = dot_exact(lower_ones, steps, NN)
    cumulative_rows = cumulative.T
    betas = sigmoid(rates)
    seg_rows = seg.T
    same = seg == seg_rows
    within = same & (row >= col)
    strict = same & (row > col)
    carry = seg == last_seen
    ends = seg == seg[CHUNK - 1 :, :]
    scales = []
    for head in range(heads):
        cum = lane_column(cumulative, head)
        cum_row = cumulative_rows[head : head + 1, :]
        gap = jnp.exp(jnp.minimum(cum - cum_row, 0.0))
        last = cum[CHUNK - 1 :, :]
        scales.append(
            dict(
                beta=lane_column(betas, heads + head),
                within=jnp.where(within, gap, 0.0),
                strict=jnp.where(strict, gap, 0.0),
                start=jnp.where(carry, jnp.exp(cum), 0.0),
                end=jnp.where(ends, jnp.exp(jnp.minimum(last - cum, 0.0)), 0.0),
                keep=jnp.where(carry[CHUNK - 1 :, :], jnp.exp(last), 0.0),
            )
        )
    return scales, steps, betas


def forward_kernel(
    heads, subs, proj_ref, seg_ref, conv_ref, rate_ref, gain_ref,
    mixed_ref, inverse_ref, w_ref, pseudo_ref, out_ref, state_ref, conv_out_ref,
    state, halo, seg_halo,
):
    step = pl.program_id(0)

    @pl.when(step == 0)
    def _():
        state[...] = jnp.zeros_like(state)
        halo[...] = jnp.zeros_like(halo)
        seg_halo[...] = jnp.full_like(seg_halo, -1.0)

    row, col = grids()
    wide = heads * WIDTH
    each = range(heads)
    items = [(sub, head) for sub in range(subs) for head in each]
    head_lanes = [slice(head * WIDTH, (head + 1) * WIDTH) for head in each]
    chunk_rows = [slice(sub * CHUNK, (sub + 1) * CHUNK) for sub in range(subs)]

    def with_halo(ref, before, sub, lanes):
        if sub:
            return ref[sub * CHUNK - HALO : (sub + 1) * CHUNK, lanes]
        return jnp.concatenate([before[:, lanes], ref[:CHUNK, lanes]], axis=0)

    keeps, scales = [], {}
    for sub in range(subs):
        seg_rows = with_halo(seg_ref, seg_halo, sub, slice(None))
        seg = seg_rows[HALO:]
        keeps.append([None] + [shifted(seg_rows, offset) == seg for offset in range(1, 4)])
        rates = proj_ref[chunk_rows[sub], 4 * wide : 4 * wide + WIDTH]
        found, _, _ = chunk_scales(
            heads, rates, rate_ref[...], seg, seg_rows[HALO - 1 : HALO, :], row, col
        )
        for head in each:
            scales[sub, head] = found[head]

    def signal(part, item):
        sub, head = item
        at = part * wide + head * WIDTH
        lanes = slice(at, at + WIDTH)
        terms = conv_terms(with_halo(proj_ref, halo, sub, lanes), keeps[sub])
        total = conv_sum(terms, conv_ref, part, head_lanes[head])
        conv_out_ref[chunk_rows[sub], lanes] = total
        return total * sigmoid(total)

    def unit(rows):
        return rows * lax.rsqrt(jnp.sum(rows * rows, axis=-1, keepdims=True) + unit_eps)

    keys = {item: signal(1, item) for item in items}
    keys = {item: unit(keys[item]) for item in items}
    keys_low = {item: keys[item].astype(bf16) for item in items}
    lowers = [
        dot(keys_low[item], keys_low[item], NT) * (scales[item]["strict"] * scales[item]["beta"])
        for item in items
    ]
    queries, scores, targets, gates, ends = {}, {}, {}, {}, {}

    def query_of(item):
        queries[item] = unit(signal(0, item)) * WIDTH**-0.5

    def scores_of(item):
        scores[item] = (
            dot(queries[item], keys_low[item], NT) * scales[item]["within"]
        ).astype(bf16)
        queries[item] = (scales[item]["start"] * queries[item]).astype(bf16)

    def target_of(item):
        beta = scales[item]["beta"]
        targets[item] = jnp.concatenate(
            [
                (beta * signal(2, item)).astype(bf16),
                (beta * scales[item]["start"] * keys[item]).astype(bf16),
            ],
            axis=1,
        )

    def gate_of(item):
        sub, head = item
        gate = proj_ref[chunk_rows[sub], 3 * wide + head * WIDTH : 3 * wide + (head + 1) * WIDTH]
        gates[item] = gain_ref[...] * gate * sigmoid(gate)
        ends[item] = (scales[item]["end"] * keys[item]).astype(bf16)

    beside = [
        functools.partial(work, item)
        for work in (query_of, target_of, scores_of, gate_of)
        for item in items
    ]
    inverses = unit_lower_inverses(lowers, row, col, beside)
    inverses = {item: inverse.astype(bf16) for item, inverse in zip(items, inverses)}
    halo[...] = proj_ref[subs * CHUNK - HALO :, : 3 * wide]
    seg_halo[...] = seg_ref[subs * CHUNK - HALO :, :]
    solved = {item: dot(inverses[item], targets[item], NN) for item in items}
    carried = {item: solved[item][:, WIDTH:].astype(bf16) for item in items}
    memories = [state[head] for head in each]
    for sub in range(subs):
        rows = chunk_rows[sub]
        reads = [
            dot(
                jnp.concatenate([carried[sub, head], queries[sub, head]], axis=0),
                memories[head],
                NN,
            )
            for head in each
        ]
        pseudos = [
            (solved[sub, head][:, :WIDTH] - reads[head][:CHUNK]).astype(bf16) for head in each
        ]
        updates = [dot(ends[sub, head], pseudos[head], TN) for head in each]
        outputs = [
            dot(scores[sub, head], pseudos[head], NN) + reads[head][CHUNK:] for head in each
        ]
        for head, lanes in enumerate(head_lanes):
            state_ref[sub, head] = memories[head]
            memories[head] = scales[sub, head]["keep"] * memories[head] + updates[head]
            inverse_ref[rows, lanes] = inverses[sub, head]
            w_ref[rows, lanes] = carried[sub, head]
            pseudo_ref[rows, lanes] = pseudos[head]
            output = outputs[head]
            out_ref[rows, lanes] = output
            inv_rms = lax.rsqrt(jnp.mean(output * output, axis=-1, keepdims=True) + norm_eps)
            mixed_ref[rows, lanes] = (output * inv_rms * gates[sub, head]).astype(bf16)
    for head in each:
        state[head] = memories[head]


def backward_kernel(
    heads, proj_ref, seg_ref, seg_before_ref, before_ref, conv_ref, rate_ref, gain_ref, grad_ref,
    inverse_ref, w_ref, pseudo_ref, out_ref, state_ref, conv_out_ref,
    dproj_ref, dconv_ref, drate_ref, dgain_ref,
    dstate, carry_halo,
):
    step = pl.program_id(0)
    first = step == pl.num_programs(0) - 1

    @pl.when(step == 0)
    def _():
        dstate[...] = jnp.zeros_like(dstate)
        carry_halo[...] = jnp.zeros_like(carry_halo)
        dconv_ref[...] = jnp.zeros_like(dconv_ref)
        drate_ref[...] = jnp.zeros_like(drate_ref)
        dgain_ref[...] = jnp.zeros_like(dgain_ref)

    row, col = grids()
    seg = seg_ref[...]
    seg_before = jnp.where(first, -1.0, seg_before_ref[...])
    seg_rows = jnp.concatenate([seg_before, seg], axis=0)
    keeps = [None] + [shifted(seg_rows, offset) == seg for offset in range(1, 4)]
    last_seen = seg_before[HALO - 1 :, :]
    wide = heads * WIDTH
    rates = proj_ref[:, 4 * wide : 4 * wide + WIDTH]
    neg_rate = rate_ref[...]
    scales, steps, betas = chunk_scales(heads, rates, neg_rate, seg, last_seen, row, col)

    def signal(part, head):
        at = part * wide + head * WIDTH
        total = conv_out_ref[:, at : at + WIDTH]
        return total, sigmoid(total)

    def signal_back(part, head, total, gate, grad):
        grad = grad * (gate * (1.0 + total * (1.0 - gate)))
        at = part * wide + head * WIDTH
        lanes = slice(at, at + WIDTH)
        head_lanes = slice(head * WIDTH, (head + 1) * WIDTH)
        rows = proj_ref[:, lanes]
        rows_before = before_ref[:, lanes]
        spread, spread_before = None, None
        for offset in range(4):
            tap = pl.ds(part * 4 + 3 - offset, 1)
            weight = conv_ref[tap, head_lanes]
            if offset:
                back = jnp.where(keeps[offset], grad, 0.0)
                back = jnp.concatenate([jnp.zeros((HALO, WIDTH), f32), back], axis=0)
                back = pltpu.roll(back, CHUNK + HALO - offset, 0)
                back_before, back = back[:HALO], back[HALO:]
                product = jnp.sum(back * rows, axis=0, keepdims=True) + jnp.sum(
                    back_before * rows_before, axis=0, keepdims=True
                )
                spread = spread + weight * back
                before = weight * back_before
                spread_before = before if spread_before is None else spread_before + before
            else:
                product = jnp.sum(grad * rows, axis=0, keepdims=True)
                spread = weight * grad
            dconv_ref[tap, head_lanes] += product
        tail = spread[CHUNK - HALO :] + carry_halo[:, lanes]
        dproj_ref[:, lanes] = jnp.concatenate([spread[: CHUNK - HALO], tail], axis=0).astype(bf16)
        carry_halo[:, lanes] = spread_before

    lane = col
    cum_columns = jnp.zeros((CHUNK, WIDTH), f32)
    cum_rows = jnp.zeros((CHUNK, CHUNK), f32)
    dbeta_columns = jnp.zeros((CHUNK, WIDTH), f32)
    dgain = jnp.zeros((1, WIDTH), f32)
    each = range(heads)
    head_lanes = [slice(head * WIDTH, (head + 1) * WIDTH) for head in each]
    gain = gain_ref[...]
    beta, start, end, keep, within, strict = (
        [scale[name] for scale in scales]
        for name in ("beta", "start", "end", "keep", "within", "strict")
    )
    memory = [state_ref[0, head] for head in each]
    dmemory = [dstate[head] for head in each]
    inverse = [inverse_ref[:, lanes] for lanes in head_lanes]
    pseudo = [pseudo_ref[:, lanes] for lanes in head_lanes]

    q_total, q_gate = zip(*[signal(0, head) for head in each])
    k_total, k_gate = zip(*[signal(1, head) for head in each])
    q_act = [total * gate for total, gate in zip(q_total, q_gate)]
    k_act = [total * gate for total, gate in zip(k_total, k_gate)]
    q_norm = [lax.rsqrt(jnp.sum(act * act, axis=-1, keepdims=True) + unit_eps) for act in q_act]
    k_norm = [lax.rsqrt(jnp.sum(act * act, axis=-1, keepdims=True) + unit_eps) for act in k_act]
    q_unit = [act * norm for act, norm in zip(q_act, q_norm)]
    key = [act * norm for act, norm in zip(k_act, k_norm)]
    query = [unit * WIDTH**-0.5 for unit in q_unit]
    both = [
        dot(jnp.concatenate([key[h].astype(bf16), query[h].astype(bf16)], axis=0), key[h], NT)
        for h in each
    ]

    dout = []
    for head, lanes in enumerate(head_lanes):
        gate_at = slice(3 * wide + head * WIDTH, 3 * wide + (head + 1) * WIDTH)
        gate = proj_ref[:, gate_at]
        gate_s = sigmoid(gate)
        gate_act = gate * gate_s
        grad = grad_ref[:, lanes].astype(f32)
        output = out_ref[:, lanes]
        inv_rms = lax.rsqrt(jnp.mean(output * output, axis=-1, keepdims=True) + norm_eps)
        unit = output * inv_rms
        grad_unit = grad * unit
        dgain = dgain + jnp.sum(grad_unit * gate_act, axis=0, keepdims=True)
        dproj_ref[:, gate_at] = (
            grad_unit * gain * (gate_s * (1.0 + gate * (1.0 - gate_s)))
        ).astype(bf16)
        dunit = grad * (gain * gate_act)
        dout.append(
            inv_rms * (dunit - unit * jnp.mean(dunit * unit, axis=-1, keepdims=True))
        )

    lower_raw = [both[h][:CHUNK] * strict[h] for h in each]
    lower = [lower_raw[h] * beta[h] for h in each]
    scores = [both[h][CHUNK:] * within[h] for h in each]
    dout_low = [value.astype(bf16) for value in dout]
    from_scores = [dot(scores[h], dout_low[h], TN) for h in each]
    from_end = [dot(end[h] * key[h], dmemory[h], NN) for h in each]
    dpseudo = [(from_scores[h] + from_end[h]).astype(bf16) for h in each]
    updates = [
        dot(
            jnp.concatenate(
                [(start[h] * query[h]).astype(bf16), -w_ref[:, head_lanes[h]]], axis=0
            ),
            jnp.concatenate([dout_low[h], dpseudo[h]], axis=0),
            TN,
        )
        for h in each
    ]
    dkey_end = [end[h] * dot(pseudo[h], dmemory[h], NT) for h in each]
    for h in each:
        dstate[h] = keep[h] * dmemory[h] + updates[h]
    solved = [dot(inverse[h], dpseudo[h], TN) for h in each]
    grads = [jnp.concatenate([dout_low[h], solved[h].astype(bf16)], axis=0) for h in each]
    reads = [dot(grads[h], memory[h], NT) for h in each]
    by_pseudo = [dot(grads[h], pseudo[h], NT) for h in each]
    near = [(-by_pseudo[h][CHUNK:] * (strict[h] * beta[h])).astype(bf16) for h in each]
    far = [(by_pseudo[h][:CHUNK] * within[h]).astype(bf16) for h in each]
    nears = [jnp.concatenate([near[h], far[h]], axis=0) for h in each]
    toward = [dot(nears[h], key[h], NN) for h in each]
    turned = [
        dot(
            nears[h],
            jnp.concatenate([key[h].astype(bf16), query[h].astype(bf16)], axis=0),
            TN,
        )
        for h in each
    ]
    dquery_start = [start[h] * reads[h][:CHUNK] for h in each]
    dkey_start = [-start[h] * reads[h][CHUNK:] for h in each]
    v_total, v_gate = zip(*[signal(2, head) for head in each])
    for h in each:
        dlower = -by_pseudo[h][CHUNK:]
        start_terms = dkey_start[h] * key[h]
        dbeta = jnp.sum(
            solved[h] * (v_total[h] * v_gate[h]) + start_terms + dlower * lower_raw[h],
            axis=-1,
            keepdims=True,
        )
        pair = by_pseudo[h][:CHUNK] * scores[h] + dlower * lower[h]
        end_terms = dkey_end[h] * key[h]
        dcum = jnp.sum(
            pair + dquery_start[h] * query[h] + start_terms * beta[h] - end_terms,
            axis=-1,
            keepdims=True,
        )
        last_total = jnp.sum(
            jnp.sum(end_terms, axis=0, keepdims=True)
            + keep[h] * jnp.sum(memory[h] * dmemory[h], axis=0, keepdims=True),
            axis=-1,
            keepdims=True,
        )
        dcum = dcum + jnp.where(row[:, :1] == CHUNK - 1, last_total, 0.0)
        cum_columns = cum_columns + jnp.where(lane == h, dcum, 0.0)
        dbeta_columns = dbeta_columns + jnp.where(lane == heads + h, dbeta, 0.0)
        cum_rows = cum_rows + jnp.where(row == h, jnp.sum(pair, axis=0, keepdims=True), 0.0)
    dkey = [
        toward[h][:CHUNK] + turned[h] + beta[h] * dkey_start[h] + dkey_end[h] for h in each
    ]
    dquery = [(toward[h][CHUNK:] + dquery_start[h]) * WIDTH**-0.5 for h in each]
    dq_act = [
        q_norm[h] * (dquery[h] - q_unit[h] * jnp.sum(q_unit[h] * dquery[h], axis=-1, keepdims=True))
        for h in each
    ]
    dk_act = [
        k_norm[h] * (dkey[h] - key[h] * jnp.sum(key[h] * dkey[h], axis=-1, keepdims=True))
        for h in each
    ]
    for h in each:
        signal_back(0, h, q_total[h], q_gate[h], dq_act[h])
        signal_back(1, h, k_total[h], k_gate[h], dk_act[h])
        signal_back(2, h, v_total[h], v_gate[h], beta[h] * solved[h])

    upper_ones = jnp.where(row <= col, 1.0, 0.0).astype(f32)
    dsteps = dot_exact(upper_ones, cum_columns - cum_rows.T, NN)
    drate_ref[...] += jnp.sum(dsteps * steps, axis=0, keepdims=True)
    dgain_ref[...] += dgain
    dlogits = dsteps * neg_rate * betas + dbeta_columns * betas * (1.0 - betas)
    dproj_ref[:, 4 * wide : 4 * wide + WIDTH] = jnp.where(
        lane < 2 * heads, dlogits, 0.0
    ).astype(bf16)


def mixer_forward(proj, seg_wide, conv_rows, neg_rate, gain):
    length, width = proj.shape
    heads = (width - WIDTH) // (4 * WIDTH)
    wide = heads * WIDTH
    count = length // CHUNK
    subs = 2 if count % 2 == 0 else 1
    by_chunk = lambda cols: pl.BlockSpec((subs * CHUNK, cols), lambda i: (i, 0))
    whole = lambda rows, cols: pl.BlockSpec((rows, cols), lambda i: (0, 0))
    return pl.pallas_call(
        functools.partial(forward_kernel, heads, subs),
        grid=(count // subs,),
        in_specs=[
            by_chunk(width), by_chunk(WIDTH), whole(12, wide), whole(1, WIDTH), whole(1, WIDTH),
        ],
        out_specs=[
            by_chunk(wide), by_chunk(wide), by_chunk(wide), by_chunk(wide), by_chunk(wide),
            pl.BlockSpec((subs, heads, WIDTH, WIDTH), lambda i: (i, 0, 0, 0)),
            by_chunk(3 * wide),
        ],
        out_shape=[
            pltpu.HBM((length, wide), bf16),
            pltpu.HBM((length, wide), bf16),
            pltpu.HBM((length, wide), bf16),
            pltpu.HBM((length, wide), bf16),
            pltpu.HBM((length, wide), f32),
            pltpu.HBM((count, heads, WIDTH, WIDTH), f32),
            pltpu.HBM((length, 3 * wide), f32),
        ],
        scratch_shapes=[
            pltpu.VMEM((heads, WIDTH, WIDTH), f32),
            pltpu.VMEM((HALO, 3 * wide), f32),
            pltpu.VMEM((HALO, WIDTH), f32),
        ],
        compiler_params=pltpu.CompilerParams(vmem_limit_bytes=48 * 1024 * 1024),
        cost_estimate=pl.CostEstimate(
            flops=2 * 160 * length * WIDTH * wide,
            bytes_accessed=4 * length * (width + 3 * wide),
            transcendentals=8 * length * wide,
        ),
        name="mixer_forward",
    )(*in_hbm(proj, seg_wide, conv_rows, neg_rate, gain))


def mixer_backward(proj, seg_wide, conv_rows, neg_rate, gain, grad, saved):
    length, width = proj.shape
    heads = (width - WIDTH) // (4 * WIDTH)
    wide = heads * WIDTH
    count = length // CHUNK
    back = lambda i: count - 1 - i
    by_chunk = lambda cols: pl.BlockSpec((CHUNK, cols), lambda i: (back(i), 0))
    before = lambda cols: pl.BlockSpec(
        (HALO, cols), lambda i: (jnp.maximum(back(i) * (CHUNK // HALO) - 1, 0), 0)
    )
    whole = lambda rows, cols: pl.BlockSpec((rows, cols), lambda i: (0, 0))
    return pl.pallas_call(
        functools.partial(backward_kernel, heads),
        grid=(count,),
        in_specs=[
            by_chunk(width), by_chunk(WIDTH), before(WIDTH), before(3 * wide),
            whole(12, wide), whole(1, WIDTH), whole(1, WIDTH),
            by_chunk(wide), by_chunk(wide), by_chunk(wide), by_chunk(wide), by_chunk(wide),
            pl.BlockSpec((1, heads, WIDTH, WIDTH), lambda i: (back(i), 0, 0, 0)),
            by_chunk(3 * wide),
        ],
        out_specs=[by_chunk(width), whole(12, wide), whole(1, WIDTH), whole(1, WIDTH)],
        out_shape=[
            pltpu.HBM((length, width), bf16),
            pltpu.HBM((12, wide), f32),
            pltpu.HBM((1, WIDTH), f32),
            pltpu.HBM((1, WIDTH), f32),
        ],
        scratch_shapes=[
            pltpu.VMEM((heads, WIDTH, WIDTH), f32),
            pltpu.VMEM((HALO, 3 * wide), f32),
        ],
        compiler_params=pltpu.CompilerParams(vmem_limit_bytes=48 * 1024 * 1024),
        cost_estimate=pl.CostEstimate(
            flops=2 * 180 * length * WIDTH * wide,
            bytes_accessed=4 * length * (2 * width + 3 * wide),
            transcendentals=8 * length * wide,
        ),
        name="mixer_backward",
    )(*in_hbm(proj, seg_wide, seg_wide, proj, conv_rows, neg_rate, gain, grad, *saved))


def project_kernel(x_ref, w_ref, out_ref):
    out_ref[...] = dot(x_ref[...], w_ref[...], NN)


def project(x, packed, columns):
    rows, model = x.shape
    return pl.pallas_call(
        project_kernel,
        grid=(pl.cdiv(columns, COLUMN_TILE),),
        in_specs=[
            pl.BlockSpec((rows, model), lambda i: (0, 0)),
            pl.BlockSpec((model, COLUMN_TILE), lambda i: (0, i)),
        ],
        out_specs=pl.BlockSpec((rows, COLUMN_TILE), lambda i: (0, i)),
        out_shape=pltpu.HBM((rows, columns), f32),
        compiler_params=pltpu.CompilerParams(vmem_limit_bytes=40 * 1024 * 1024),
        cost_estimate=pl.CostEstimate(
            flops=2 * rows * model * columns,
            bytes_accessed=2 * model * (rows + columns) + 4 * rows * columns,
            transcendentals=0,
        ),
        name="project",
    )(*in_hbm(x, packed))


def ffn_kernel(tiles, x_ref, dy_ref, w_ref, h_ref, g_ref, y_ref, dx_ref, y_sum, dx_sum):
    step = pl.program_id(0)

    @pl.when(step == 0)
    def _():
        y_sum[...] = jnp.zeros_like(y_sum)
        dx_sum[...] = jnp.zeros_like(dx_sum)

    def units(size):
        gate_up = dot(x_ref[...], w_ref[:, : 2 * size], NN)
        grad = dot(dy_ref[...], w_ref[:, 2 * size : 3 * size], NN)
        gate, up = gate_up[:, :size], gate_up[:, size:]
        gate_s = sigmoid(gate)
        act = gate * gate_s
        h_ref[:, :size] = (act * up).astype(bf16)
        g_ref[:, :size] = (grad * up * (gate_s + act * (1.0 - gate_s))).astype(bf16)
        g_ref[:, size : 2 * size] = (grad * act).astype(bf16)
        y_sum[...] += dot(h_ref[:, :size], w_ref[:, 2 * size : 3 * size], NT)
        dx_sum[...] += dot(g_ref[:, : 2 * size], w_ref[:, : 2 * size], NT)

    per_tile(tiles, step, units)

    @pl.when(step == len(tiles) - 1)
    def _():
        y_ref[...] = y_sum[...].astype(bf16)
        dx_ref[...] = dx_sum[...].astype(bf16)


def per_tile(tiles, step, units):
    if tiles[0] == tiles[-1]:
        units(tiles[0])
        return

    @pl.when(step < len(tiles) - 1)
    def _():
        units(tiles[0])

    @pl.when(step == len(tiles) - 1)
    def _():
        units(tiles[-1])


def ffn(x, dy, packed, tiles):
    rows, model = x.shape
    hidden = sum(tiles)
    whole = pl.BlockSpec((rows, model), lambda i: (0, 0))
    return pl.pallas_call(
        functools.partial(ffn_kernel, tiles),
        grid=(len(tiles),),
        in_specs=[whole, whole, pl.BlockSpec((model, 3 * tiles[0]), lambda i: (0, i))],
        out_specs=[
            pl.BlockSpec((rows, tiles[0]), lambda i: (0, i)),
            pl.BlockSpec((rows, 2 * tiles[0]), lambda i: (0, i)),
            whole,
            whole,
        ],
        out_shape=[
            pltpu.HBM((rows, hidden), bf16),
            pltpu.HBM((rows, 2 * hidden), bf16),
            pltpu.HBM((rows, model), bf16),
            pltpu.HBM((rows, model), bf16),
        ],
        scratch_shapes=[pltpu.VMEM((rows, model), f32), pltpu.VMEM((rows, model), f32)],
        compiler_params=pltpu.CompilerParams(vmem_limit_bytes=48 * 1024 * 1024),
        cost_estimate=pl.CostEstimate(
            flops=12 * rows * model * hidden,
            bytes_accessed=2 * (3 * model * hidden + rows * (4 * model + 3 * hidden)),
            transcendentals=rows * hidden,
        ),
        name="ffn",
    )(*in_hbm(x, dy, packed))


def ffn_grads_kernel(tiles, *refs):
    *inputs, out_ref, x_turned, dy_turned = refs
    count = len(inputs) // 4
    xs, dys, hs, gs = (inputs[at * count : (at + 1) * count] for at in range(4))
    step = pl.program_id(0)
    ends = [0]
    for x_ref in xs:
        ends.append(ends[-1] + x_ref.shape[0])
    lanes = [slice(first, last) for first, last in zip(ends, ends[1:])]

    @pl.when(step == 0)
    def _():
        for at, x_ref, dy_ref in zip(lanes, xs, dys):
            x_turned[:, at] = x_ref[...].T
            dy_turned[:, at] = dy_ref[...].T

    def units(size):
        up_grad, down_grad = 0.0, 0.0
        for at, h_ref, g_ref in zip(lanes, hs, gs):
            up_grad = up_grad + dot(x_turned[:, at], g_ref[:, : 2 * size], NN)
            down_grad = down_grad + dot(dy_turned[:, at], h_ref[:, :size], NN)
        out_ref[:, : 2 * size] = up_grad.astype(bf16)
        out_ref[:, 2 * size : 3 * size] = down_grad.astype(bf16)

    per_tile(tiles, step, units)


def ffn_grads(xs, dys, hs, gs, tiles):
    model = xs[0].shape[1]
    hidden = sum(tiles)
    total = sum(x.shape[0] for x in xs)
    whole = [pl.BlockSpec(x.shape, lambda i: (0, 0)) for x in xs]
    return pl.pallas_call(
        functools.partial(ffn_grads_kernel, tiles),
        grid=(len(tiles),),
        in_specs=whole
        + whole
        + [pl.BlockSpec((x.shape[0], tiles[0]), lambda i: (0, i)) for x in xs]
        + [pl.BlockSpec((x.shape[0], 2 * tiles[0]), lambda i: (0, i)) for x in xs],
        out_specs=pl.BlockSpec((model, 3 * tiles[0]), lambda i: (0, i)),
        out_shape=pltpu.HBM((model, 3 * hidden), bf16),
        scratch_shapes=[pltpu.VMEM((model, total), bf16), pltpu.VMEM((model, total), bf16)],
        compiler_params=pltpu.CompilerParams(vmem_limit_bytes=48 * 1024 * 1024),
        cost_estimate=pl.CostEstimate(
            flops=6 * total * model * hidden,
            bytes_accessed=2 * (3 * model * hidden + total * (2 * model + 3 * hidden)),
            transcendentals=0,
        ),
        name="ffn_grads",
    )(*in_hbm(*xs, *dys, *hs, *gs))


def mixer_grads_kernel(
    orders, split, main_steps, core_ref, normed_ref, residual_ref, dproj_ref, mixed_ref, conv_ref,
    first_sent_ref, first_kept_ref, second_sent_ref, second_kept_ref,
    turned, residual_turned, conv_turned,
):
    step = pl.program_id(0)
    last = pl.num_programs(0) - 1
    first_order, second_order = orders
    count = len(first_order)
    size = normed_ref.shape[1] // count

    @pl.when(step == 0)
    def _():
        normed = normed_ref[...].T
        residual = residual_ref[...].T
        for at, block in enumerate(first_order):
            away = (block % 2 + 1 + core_ref[0]) % 2
            begin = (away * (count // 2) + at % (count // 2)) * size
            rows = pl.ds(pl.multiple_of(begin, size), size)
            from_rows = slice(block * size, (block + 1) * size)
            turned[rows, :] = normed[from_rows]
            residual_turned[rows, :] = residual[from_rows]
            conv_turned[rows, :] = conv_ref[from_rows, :]

    def store(grads, lanes):
        grads = grads.astype(bf16)
        half = count // 2 * size

        @pl.when(step < split)
        def _():
            first_sent_ref[:, lanes] = grads[:half]
            first_kept_ref[:, lanes] = grads[half:]

        @pl.when(step >= split)
        def _():
            for to, block in enumerate(second_order[: count // 2]):
                at = first_order.index(block)
                to_rows = slice(to * size, (to + 1) * size)
                second_sent_ref[to_rows, lanes] = grads[at * size : (at + 1) * size]
                second_kept_ref[to_rows, lanes] = grads[half + at * size : half + (at + 1) * size]

    @pl.when(step < main_steps)
    def _():
        store(dot(turned[...], dproj_ref[...], NN), slice(None))

    @pl.when((step >= main_steps) & (step < last))
    def _():
        store(dot(residual_turned[...], mixed_ref[...], NN), slice(None))

    @pl.when(step == last)
    def _():
        store(dot(turned[...], dproj_ref[:, :WIDTH], NN) + conv_turned[...], slice(0, WIDTH))


def mixer_grads(normed, residual, dproj, mixed, conv_block, core, orders):
    rows, model = normed.shape
    wide = mixed.shape[1]
    tile = 2 * WIDTH if wide % (2 * WIDTH) == 0 else WIDTH
    main_steps = 4 * wide // tile
    out_steps = wide // tile
    columns = 5 * wide + WIDTH
    split = (main_steps + out_steps + 1) * 5 // 9
    first = split * tile
    whole = lambda cols: pl.BlockSpec((rows, cols), lambda i, core: (0, 0))
    first_block = pl.BlockSpec((model // 2, tile), lambda i, core: (0, jnp.minimum(i, split - 1)))
    second_block = pl.BlockSpec((model // 2, tile), lambda i, core: (0, jnp.maximum(i - split, 0)))
    first_shape = pltpu.HBM((model // 2, first), bf16)
    second_shape = pltpu.HBM((model // 2, columns - first), bf16)
    return pl.pallas_call(
        functools.partial(mixer_grads_kernel, orders, split, main_steps),
        grid_spec=pltpu.PrefetchScalarGridSpec(
            num_scalar_prefetch=1,
            grid=(main_steps + out_steps + 1,),
            in_specs=[
                whole(model),
                whole(model),
                pl.BlockSpec((rows, tile), lambda i, core: (0, jnp.minimum(i, main_steps))),
                pl.BlockSpec(
                    (rows, tile), lambda i, core: (0, jnp.clip(i - main_steps, 0, out_steps - 1))
                ),
                pl.BlockSpec((model, WIDTH), lambda i, core: (0, 0)),
            ],
            out_specs=[first_block, first_block, second_block, second_block],
            scratch_shapes=[
                pltpu.VMEM((model, rows), bf16),
                pltpu.VMEM((model, rows), bf16),
                pltpu.VMEM((model, WIDTH), f32),
            ],
        ),
        out_shape=[first_shape, first_shape, second_shape, second_shape],
        compiler_params=pltpu.CompilerParams(vmem_limit_bytes=40 * 1024 * 1024),
        cost_estimate=pl.CostEstimate(
            flops=2 * rows * model * columns,
            bytes_accessed=2 * (2 * rows * model + (rows + model) * columns),
            transcendentals=0,
        ),
        name="mixer_grads",
    )(core, *in_hbm(normed, residual, dproj, mixed, conv_block))


def rms_norm(values, scales):
    return values * lax.rsqrt(jnp.mean(values * values, axis=-1, keepdims=True) + norm_eps) * scales


def first_norm(values, gains):
    return rms_norm(values, gains[0])


def second_norm(values, gains):
    return rms_norm(values, gains[1])


def contract_last(operand, other):
    return lax.dot_general(
        operand, other, (((1,), (1,)), ((), ())), preferred_element_type=jnp.float32
    )


def contract_first(operand, other):
    return lax.dot_general(
        operand, other, (((0,), (0,)), ((), ())), preferred_element_type=jnp.float32
    )


def swap(rows):
    return lax.ppermute(rows, "tensor", [(0, 1), (1, 0)])


def sum_over(values, axis):
    size = lax.axis_size(axis)
    if size & (size - 1):
        return lax.psum(values, axis)
    bit = 1
    while bit < size:
        values = values + lax.ppermute(values, axis, [(i, i ^ bit) for i in range(size)])
        bit *= 2
    return values


def hidden_tiles(hidden):
    if hidden % WIDTH:
        return (hidden,)
    return (2 * WIDTH,) * (hidden // (2 * WIDTH)) + (WIDTH,) * (hidden // WIDTH % 2)


def pack_tiles(gate, up, down, tiles):
    blocks = []
    at = 0
    for size in tiles:
        blocks += [part[:, at : at + size] for part in (gate, up, down)]
        at += size
    return jnp.concatenate(blocks, axis=1)


def unpack_tiles(packed, tiles):
    parts = ([], [], [])
    at = 0
    for size in tiles:
        for part in parts:
            part.append(packed[:, at : at + size])
            at += size
    return [jnp.concatenate(part, axis=1) for part in parts]


def ffn_plain(x, dy, packed, tiles):
    gate_w, up_w, down_w = unpack_tiles(packed, tiles)
    gate = jnp.dot(x, gate_w, preferred_element_type=f32)
    up = jnp.dot(x, up_w, preferred_element_type=f32)
    grad = jnp.dot(dy, down_w, preferred_element_type=f32)
    gate_s = sigmoid(gate)
    act = gate * gate_s
    hidden = (act * up).astype(bf16)
    gate_grad = (grad * up * (gate_s + act * (1.0 - gate_s))).astype(bf16)
    up_grad = (grad * act).astype(bf16)
    share = contract_last(hidden, down_w).astype(bf16)
    dx = (contract_last(gate_grad, gate_w) + contract_last(up_grad, up_w)).astype(bf16)
    return hidden, jnp.concatenate([gate_grad, up_grad], axis=1), share, dx


def ffn_grads_plain(x, dy, hidden, grads, tiles):
    size = hidden.shape[1]
    return pack_tiles(
        contract_first(x, grads[:, :size]).astype(bf16),
        contract_first(x, grads[:, size:]).astype(bf16),
        contract_first(dy, hidden).astype(bf16),
        tiles,
    )


def bit_orders(size):
    bits = list(range(size.bit_length() - 1))
    return bits, bits[:1] + bits[2:] + bits[1:2]


def block_order(size, bits):
    return sorted(range(size), key=lambda i: [(i >> bit) & 1 for bit in bits])


def outgoing(terms, bit):
    mine = lax.axis_index("dp") >> bit & 1
    half = terms[0].shape[0] // 2
    total = 0.0
    for term in terms:
        total = total + lax.dynamic_slice_in_dim(term, (1 - mine) * half, half).astype(f32)
    return total.astype(bf16)


def settle(terms, bit, sent):
    mine = lax.axis_index("dp") >> bit & 1
    half = terms[0].shape[0] // 2
    own = [lax.dynamic_slice_in_dim(term, mine * half, half) for term in terms]
    return own + [flip(sent, bit)]


def flip(values, bit):
    size = lax.axis_size("dp")
    return lax.ppermute(values, "dp", [(i, i ^ (1 << bit)) for i in range(size)])


def local(
    tokens,
    segment_ids,
    norm_gains,
    w_mixer_in,
    w_rates,
    conv_weight,
    a_log,
    out_gain,
    w_output,
    w_gate_up,
    w_down,
    cotangent,
):
    dp_size = lax.axis_size("dp")
    pair = lax.axis_size("tensor") == 2
    tensor_rank = lax.axis_index("tensor")
    rows_here, _, heads, _ = w_mixer_in.shape
    model_width = rows_here * dp_size
    wide = heads * WIDTH
    hidden_here = w_gate_up.shape[2]
    tiles = hidden_tiles(hidden_here)
    kernels = hidden_here % WIDTH == 0
    taps_here = conv_weight.shape[3]
    own_rows = tokens.shape[1]
    projected_width = 4 * wide + WIDTH

    def gather_rows(rows):
        return lax.all_gather(rows, "tensor", axis=0, tiled=True)

    def scatter_rows(product):
        return lax.psum_scatter(product.astype(bf16), "tensor", scatter_dimension=0, tiled=True)

    def in_order(own, other):
        first = tensor_rank == 0
        return jnp.concatenate([jnp.where(first, own, other), jnp.where(first, other, own)], axis=0)

    def own_and_other(rows):
        own = lax.dynamic_slice_in_dim(rows, tensor_rank * own_rows, own_rows)
        return own, lax.dynamic_slice_in_dim(rows, (1 - tensor_rank) * own_rows, own_rows)

    conv_block = jnp.pad(
        conv_weight.transpose(3, 0, 1, 2).reshape(taps_here, 12 * heads),
        ((0, rows_here - taps_here), (0, WIDTH - 14 * heads)),
    )
    mixer_pack = jnp.concatenate(
        [
            w_mixer_in.reshape(rows_here, -1),
            w_rates.reshape(rows_here, -1),
            conv_block,
            w_output.T,
        ],
        axis=1,
    )
    mix_full = lax.all_gather(mixer_pack, "dp", axis=0, tiled=True)
    ffn_pack = pack_tiles(w_gate_up[:, 0], w_gate_up[:, 1], w_down.T, tiles)
    ffn_full = lax.all_gather(ffn_pack, "dp", axis=0, tiled=True)
    out_mine = mix_full[:, projected_width:]
    conv_at = 4 * wide + 2 * heads
    conv_rows = (
        mix_full[:, conv_at : conv_at + 12 * heads]
        .reshape(dp_size, rows_here, 12 * heads)[:, :taps_here]
        .reshape(dp_size * taps_here, 12 * heads)
        .T.reshape(12, wide)
        .astype(f32)
    )
    segment = jnp.broadcast_to(segment_ids[0][:, None].astype(f32), (segment_ids.shape[1], WIDTH))
    neg_rate = jnp.pad(
        -jnp.exp(lax.dynamic_slice_in_dim(a_log, tensor_rank * heads, heads)), (0, WIDTH - heads)
    )[None]
    gain_row = out_gain[None]

    grad_own = cotangent[0]
    inputs = tokens[0].astype(f32)
    normed, first_back = jax.vjp(first_norm, inputs, norm_gains)
    normed = normed.astype(bf16)
    if pair:
        normed_other = swap(normed)
        grad_sent, normed_other = lax.optimization_barrier((grad_own, normed_other))
        grad_other = swap(grad_sent)
        normed_all, grad_other, out_sent = lax.optimization_barrier(
            (in_order(normed, normed_other), grad_other, out_mine)
        )
        out_other = swap(out_sent)
    else:
        normed_all = gather_rows(normed)
    projected = project(normed_all, mix_full, projected_width)
    mixed, *saved = mixer_forward(projected, segment, conv_rows, neg_rate, gain_row)
    if pair:
        mixed, out_other = lax.optimization_barrier((mixed, out_other))
        mixed_own, mixed_theirs = own_and_other(mixed)
        share = contract_last(mixed_own, out_mine) + contract_last(swap(mixed_theirs), out_other)
    else:
        share = scatter_rows(contract_last(mixed, out_mine)).astype(f32)
    residual = inputs + share
    normed_ffn, second_back = jax.vjp(second_norm, residual, norm_gains)
    normed_ffn = normed_ffn.astype(bf16)
    one_ffn = ffn if kernels else ffn_plain
    if pair:
        half = own_rows // 2
        x_others = [swap(normed_ffn[:half]), swap(normed_ffn[half:])]
        others = []
        for at, x_other in enumerate(x_others):
            others.append(one_ffn(x_other, grad_other[at * half : (at + 1) * half], ffn_full, tiles))
        received = [swap(other[3]) for other in others]
        done = [one_ffn(normed_ffn, grad_own, ffn_full, tiles)] + others
        x_parts = [normed_ffn] + x_others
        dy_parts = [grad_own, grad_other[:half], grad_other[half:]]
        dx = done[0][3].astype(f32) + jnp.concatenate(received, axis=0).astype(f32)
    else:
        x_parts = [gather_rows(normed_ffn)]
        dy_parts = [gather_rows(grad_own)]
        done = [one_ffn(x_parts[0], dy_parts[0], ffn_full, tiles)]
        dx = scatter_rows(done[0][3]).astype(f32)
    h_parts, g_parts, y_parts, _ = zip(*done)
    if kernels:
        ffn_sums = ffn_grads(x_parts, dy_parts, h_parts, g_parts, tiles)
    else:
        ffn_sums = ffn_grads_plain(x_parts[0], dy_parts[0], h_parts[0], g_parts[0], tiles)
    residual_part, second_gains = second_back(dx)
    residual_grad = grad_own.astype(f32) + residual_part
    residual_low = residual_grad.astype(bf16)
    if pair:
        grad_theirs = jnp.dot(residual_low, out_other, preferred_element_type=f32).astype(bf16)
        grad_mine = jnp.dot(residual_low, out_mine, preferred_element_type=f32).astype(bf16)
        mixed_grad = in_order(grad_mine, swap(grad_theirs))
        mixed_grad, ffn_sums, residual_sent, y_sent = lax.optimization_barrier(
            (mixed_grad, ffn_sums, residual_low, jnp.concatenate(y_parts[1:], axis=0))
        )
        residual_all = in_order(residual_low, swap(residual_sent))
    else:
        residual_all = gather_rows(residual_low)
        mixed_grad = jnp.dot(residual_all, out_mine, preferred_element_type=f32).astype(bf16)
    ffn_owned = lax.psum_scatter(ffn_sums, "dp", scatter_dimension=0, tiled=True)
    projection_grad, conv_grad, log_grad, gain_grad = mixer_backward(
        projected, segment, conv_rows, neg_rate, gain_row, mixed_grad, saved
    )
    conv_grad = jnp.pad(
        conv_grad.reshape(12 * heads, WIDTH).T.reshape(dp_size, taps_here, 12 * heads),
        ((0, 0), (0, rows_here - taps_here), (2 * heads, WIDTH - 14 * heads)),
    ).reshape(model_width, WIDTH)
    core = lax.axis_index("dp") % 2
    bits = bit_orders(dp_size)
    orders = [block_order(dp_size, order) for order in bits]
    mix_rows = mix_full[:, :projected_width]
    if pair:
        grad_here, grad_there = own_and_other(projection_grad)
        sent = contract_last(grad_there, mix_rows).astype(bf16)
        sent, projection_grad = lax.optimization_barrier((sent, projection_grad))
        half = own_rows // 2
        received, received_late = swap(sent[:half]), swap(sent[half:])
    else:
        received = scatter_rows(contract_last(projection_grad, mix_rows))
    first_sent, first_kept, second_sent, second_kept = mixer_grads(
        normed_all, residual_all, projection_grad, mixed, conv_grad, core[None], orders
    )
    if pair:
        first_sent, second_sent, received = lax.optimization_barrier(
            (first_sent, second_sent, received)
        )
    second = [second_kept, flip(second_sent, 0)]
    first = [first_kept, flip(first_sent, 0)]
    second_out = outgoing(second, bits[1][1])
    first_out = outgoing(first, bits[0][1])
    if pair:
        received_late, y_sent, _, _ = lax.optimization_barrier(
            (received_late, y_sent, first_out, second_out)
        )
        received = jnp.concatenate([received, received_late], axis=0)
        y_other = swap(y_sent)
    else:
        y_other = scatter_rows(y_parts[0])
    second = settle(second, bits[1][1], second_out)
    first = settle(first, bits[0][1], first_out)
    mixer_input_grad = received.astype(f32)
    y = y_other.astype(f32)
    if pair:
        mixer_input_grad = mixer_input_grad + contract_last(grad_here, mix_rows)
        y = y + y_parts[0].astype(f32)
    out_tokens = (residual + y).astype(bf16)[None]
    input_part, first_gains = first_back(mixer_input_grad)
    input_grad = (residual_grad + input_part).astype(bf16)[None]
    log_full = lax.dynamic_update_slice_in_dim(
        jnp.zeros(a_log.shape, f32), log_grad[0, :heads], tensor_rank * heads, 0
    )
    small = jnp.concatenate(
        [
            (first_gains + second_gains).reshape(-1, WIDTH),
            gain_grad,
            jnp.pad(log_full, (0, WIDTH - log_full.shape[0]))[None],
        ]
    )
    for one, other in zip(bits[0][2:], bits[1][2:]):
        second_out = outgoing(second, other)
        first_out = outgoing(first, one)
        if one == bits[0][2]:
            small, _ = lax.optimization_barrier((small, first_out))
        second = settle(second, other, second_out)
        first = settle(first, one, first_out)
    mix_owned = jnp.concatenate(
        [sum(term.astype(f32) for term in terms) for terms in (first, second)], axis=1
    )
    small = sum_over(sum_over(small, "dp"), "tensor")
    gain_rows = 2 * model_width // WIDTH
    gate_grad, up_grad, down_grad = unpack_tiles(ffn_owned, tiles)
    rates = mix_owned[:, 5 * wide :]
    return (
        out_tokens,
        input_grad,
        small[:gain_rows].reshape(2, model_width),
        mix_owned[:, : 4 * wide].reshape(w_mixer_in.shape),
        rates[:, : 2 * heads].reshape(w_rates.shape),
        rates[:taps_here, 2 * heads : 14 * heads]
        .reshape(taps_here, 3, 4, heads)
        .transpose(1, 2, 3, 0),
        small[gain_rows + 1, : a_log.shape[0]],
        small[gain_rows],
        mix_owned[:, 4 * wide : 5 * wide].T,
        jnp.stack([gate_grad, up_grad], axis=1).astype(f32),
        down_grad.T.astype(f32),
    )


def solution(mesh):
    in_specs = (
        P("dp", "tensor", None),
        P("dp", None),
        P(),
        P("dp", None, "tensor", None),
        P("dp", None, "tensor"),
        P(None, None, "tensor", "dp"),
        P(),
        P(),
        P("tensor", "dp"),
        P("dp", None, "tensor"),
        P("tensor", "dp"),
        P("dp", "tensor", None),
    )
    out_specs = (
        P("dp", "tensor", None),
        P("dp", "tensor", None),
        P(),
        P("dp", None, "tensor", None),
        P("dp", None, "tensor"),
        P(None, None, "tensor", "dp"),
        P(),
        P(),
        P("tensor", "dp"),
        P("dp", None, "tensor"),
        P("tensor", "dp"),
    )
    return jax.shard_map(local, mesh=mesh, in_specs=in_specs, out_specs=out_specs, check_vma=False)
```

profile of v0, /device:TPU:0, one launch (start us, length us, event | category | flops | bytes accessed | tf_op | source)
XLA Modules:
  0.0 378.1 jit_solution(3317017209501253463)
XLA Ops:
  14.1 3.0 collective-permute-start
  17.1 23.2 %collective-permute-done = bf16[512,1024]{1,0:T(8,128)(2,1)S(1)} collective-permute-done((bf16[512,1024]{1,0:T(8,128)(2,1)S(1)}, bf16[512,1024]{1,0:T(8,128)(2,1)S(1)}, u32[]{:S(2)}, u32[]{:S(2)}) %collective-permute-start) | collective-permute-done | bytes 1048608 | tf_op jit(solution)/shard_map/ppermute | solution.py:833
  44.7 27.2 %all-gather.3.cloned.1.call-done.w_ref = bf16[1024,2688]{1,0:T(8,128)(2,1)} async-done(((bf16[64,2688]{1,0:T(8,128)(2,1)}), bf16[1024,2688]{1,0:T(8,128)(2,1)}) %all-gather.3.cloned.1.call-update) | async-done | bytes 5505040 | tf_op jit(solution)/shard_map/all_gather | solution.py:981
  76.5 12.7 %project.1.proj_ref.before_ref = f32[1024,2176]{1,0:T(8,128)} custom-call(bf16[1024,1024]{1,0:T(8,128)(2,1)} %pad_maximum_fusion.x_ref.normed_ref, bf16[1024,2688]{1,0:T(8,128)(2,1)} %all-gather.3.cloned.1.call-done.w_ref), custom_call_target="tpu_custom_call" | custom-call | flops 4563402752 | bytes 15466496 | tf_op jit(solution)/shard_map/project/pallas_call | solution.py:564
  90.2 20.8 %mixer_forward.1 = (bf16[1024,512]{1,0:T(8,128)(2,1)}, bf16[1024,512]{1,0:T(8,128)(2,1)}, bf16[1024,512]{1,0:T(8,128)(2,1)}, bf16[1024,512]{1,0:T(8,128)(2,1)}, ...) custom-call(f32[1024,2176]{1,0:T(8,128)} %project.1.proj_ref.before_ref, ...), custom_call_target="tpu_custom_call" | custom-call | flops 21474836480 | bytes 15204352 | tf_op jit(solution)/shard_map/mixer_forward/pallas_call | solution.py:481
  113.0 13.3 %collective-permute-done.3 = bf16[512,512]{1,0:T(8,128)(2,1)S(1)} collective-permute-done((bf16[512,512]{1,0:T(8,128)(2,1)S(1)}, bf16[512,512]{1,0:T(8,128)(2,1)S(1)}, u32[]{:S(2)}, u32[]{:S(2)}) %collective-permute-start.3) | collective-permute-done | bytes 524320 | tf_op jit(solution)/shard_map/ppermute | solution.py:833
  134.9 10.7 %collective-permute-done.4.x_ref.refs_1_ = bf16[256,1024]{1,0:T(8,128)(2,1)} collective-permute-done((bf16[256,1024]{1,0:T(8,128)(2,1)S(1)}, bf16[256,1024]{1,0:T(8,128)(2,1)}, u32[]{:S(2)}, u32[]{:S(2)}) %collective-permute-start.4) | collective-permute-done | bytes 524320 | tf_op jit(solution)/shard_map/ppermute | solution.py:833
  145.6 4.4 %all-gather.5.cloned.1.call-done.w_ref = bf16[1024,4224]{1,0:T(8,128)(2,1)} async-done(((bf16[64,4224]{1,0:T(8,128)(2,1)}), bf16[1024,4224]{1,0:T(8,128)(2,1)}) %all-gather.5.cloned.1.call-update) | async-done | bytes 8650768 | tf_op jit(solution)/shard_map/all_gather | solution.py:983
  150.0 10.2 %ffn.4 = (bf16[256,1408]{1,0:T(8,128)(2,1)}, bf16[256,2816]{1,0:T(8,128)(2,1)}, bf16[256,1024]{1,0:T(8,128)(2,1)}, bf16[256,1024]{1,0:T(8,128)(2,1)}) custom-call(bf16[256,1024]{1,0:T(8,128)(2,1)} %collective-permute-done.4.x_ref.refs_1_, bf16[256,1024]{1,0:T(8,128)(2,1)} %get-tuple-element.139.dy_ref.refs_4_, ...), custom_call_target="tpu_custom_call" | custom-call | flops 4429185024 | bytes 12910592 | tf_op jit(solution)/shard_map/ffn/pallas_call | solution.py:629
  161.7 10.2 %ffn.5 = (bf16[256,1408]{1,0:T(8,128)(2,1)}, bf16[256,2816]{1,0:T(8,128)(2,1)}, bf16[256,1024]{1,0:T(8,128)(2,1)}, bf16[256,1024]{1,0:T(8,128)(2,1)}) custom-call(bf16[256,1024]{1,0:T(8,128)(2,1)} %collective-permute-done.6.x_ref.refs_2_, bf16[256,1024]{1,0:T(8,128)(2,1)} %get-tuple-element.140.dy_ref.refs_5_, ...), custom_call_target="tpu_custom_call" | custom-call | flops 4429185024 | bytes 12910592 | tf_op jit(solution)/shard_map/ffn/pallas_call | solution.py:629
  174.7 14.8 %ffn.3 = (bf16[512,1408]{1,0:T(8,128)(2,1)}, bf16[512,2816]{1,0:T(8,128)(2,1)}, bf16[512,1024]{1,0:T(8,128)(2,1)}, bf16[512,1024]{1,0:T(8,128)(2,1)}) custom-call(bf16[512,1024]{1,0:T(8,128)(2,1)} %copy-done.5, bf16[512,1024]{1,0:T(8,128)(2,1)} %bitcast.70, bf16[1024,4224]{1,0:T(8,128)(2,1)} %all-gather.5.cloned.1.call-done.w_ref), custom_call_target="tpu_custom_call" | custom-call | flops 8858370048 | bytes 17170432 | tf_op jit(solution)/shard_map/ffn/pallas_call | solution.py:629
  197.7 15.7 %ffn_grads.1 = bf16[1024,4224]{1,0:T(8,128)(2,1)} custom-call(bf16[512,1024]{1,0:T(8,128)(2,1)} %copy-done.5, bf16[256,1024]{1,0:T(8,128)(2,1)} %collective-permute-done.4.x_ref.refs_1_, bf16[256,1024]{1,0:T(8,128)(2,1)} %collective-permute-done.6.x_ref.refs_2_, bf16[512,1024]{1,0:T(8,128)(2,1)} %bitcast.71, ...), custom_call_target="tpu_custom_call" | custom-call | flops 8858370048 | bytes 21495808 | tf_op jit(solution)/shard_map/ffn_grads/pallas_call | solution.py:688
  217.5 28.1 %mixer_backward.1 = (bf16[1024,2176]{1,0:T(8,128)(2,1)}, f32[12,512]{1,0:T(8,128)}, f32[1,128]{1,0:T(1,128)}, f32[1,128]{1,0:T(1,128)}) custom-call(f32[1024,2176]{1,0:T(8,128)} %project.1.proj_ref.before_ref, f32[1024,128]{1,0:T(8,128)} %broadcast_in_dim.33.seg_ref.seg_before_ref, f32[1024,128]{1,0:T(8,128)} %broadcast_in_dim.33.seg_ref.seg_before_ref, ...), custom_call_target="tpu_custom_call" | custom-call | flops 24159191040 | bytes 24117248 | tf_op jit(solution)/shard_map/mixer_backward/pallas_call | solution.py:527
  245.7 7.1 %fusion.16 = bf16[512,1024]{1,0:T(8,128)(2,1)} fusion(bf16[1024,2688]{1,0:T(8,128)(2,1)} %all-gather.3.cloned.1.call-done.w_ref, bf16[1024,2176]{1,0:T(8,128)(2,1)} %get-tuple-element.87.dproj_ref, s32[]{:T(128)S(6)} %select_n.136), kind=kOutput, calls=%fused_computation.33 | convolution fusion | flops 2282225664 | bytes 7733252 | tf_op jit(solution)/shard_map/dot_general | solution.py:821
  260.4 15.6 %mixer_grads.1 = (bf16[512,1536]{1,0:T(8,128)(2,1)}, bf16[512,1536]{1,0:T(8,128)(2,1)}, bf16[512,1152]{1,0:T(8,128)(2,1)}, bf16[512,1152]{1,0:T(8,128)(2,1)}) custom-call(s32[1]{0:T(128)} %bitcast.18.core_ref, bf16[1024,1024]{1,0:T(8,128)(2,1)} %pad_maximum_fusion.x_ref.normed_ref, bf16[1024,1024]{1,0:T(8,128)(2,1)} %pad_maximum_fusion.1.residual_ref, ...), custom_call_target="tpu_custom_call" | custom-call | flops 5637144576 | bytes 15204352 | tf_op jit(solution)/shard_map/mixer_grads/pallas_call | solution.py:776
  277.5 4.0 %collective-permute-done.13 = bf16[512,1152]{1,0:T(8,128)(2,1)} collective-permute-done((bf16[512,1152]{1,0:T(8,128)(2,1)}, bf16[512,1152]{1,0:T(8,128)(2,1)}, u32[]{:S(2)}, u32[]{:S(2)}) %collective-permute-start.13) | collective-permute-done | bytes 1179680 | tf_op jit(solution)/shard_map/ppermute | solution.py:924
  286.9 3.8 %collective-permute-done.9 = bf16[256,1024]{1,0:T(8,128)(2,1)S(1)} collective-permute-done((bf16[256,1024]{1,0:T(8,128)(2,1)}, bf16[256,1024]{1,0:T(8,128)(2,1)S(1)}, u32[]{:S(2)}, u32[]{:S(2)}) %collective-permute-start.9) | collective-permute-done | bytes 524320 | tf_op jit(solution)/shard_map/ppermute | solution.py:833
  290.7 7.5 %fusion.9 = (f32[1024]{0:T(1024)S(1)}, f32[512]{0:T(512)S(1)}, f32[512,1024]{1,0:T(8,128)}) fusion(bf16[1,512,1024]{2,1,0:T(8,128)(2,1)S(1)} %copy-done, f32[512]{0:T(512)S(1)} %fusion.27, bf16[256,1024]{1,0:T(8,128)(2,1)S(1)} %collective-permute-done.9, bf16[256,1024]{1,0:T(8,128)(2,1)} %collective-permute-done.11, f32[1024]{0:T(1024)S(1)} %bitcast.90, ...), kind=kOutput, calls=%fused_computation.16 | convolution fusion | flops 2287991296 | bytes 10891268 | tf_op jit(solution)/shard_map/dot_general | solution.py:821
  302.4 6.7 %collective-permute-done.15 = bf16[256,1536]{1,0:T(8,128)(2,1)} collective-permute-done((bf16[256,1536]{1,0:T(8,128)(2,1)}, bf16[256,1536]{1,0:T(8,128)(2,1)}, u32[]{:S(2)}, u32[]{:S(2)}) %collective-permute-start.15) | collective-permute-done | bytes 786464 | tf_op jit(solution)/shard_map/ppermute | solution.py:924
  312.5 17.3 %collective-permute-done.24 = bf16[128,1152]{1,0:T(8,128)(2,1)S(1)} collective-permute-done((bf16[128,1152]{1,0:T(8,128)(2,1)S(1)}, bf16[128,1152]{1,0:T(8,128)(2,1)S(1)}, u32[]{:S(2)}, u32[]{:S(2)}) %collective-permute-start.24) | collective-permute-done | bytes 294944 | tf_op jit(solution)/shard_map/ppermute | solution.py:924
  332.3 3.3 fusion.22
  346.0 5.5 %collective-permute-done.21 = bf16[128,1536]{1,0:T(8,128)(2,1)S(1)} collective-permute-done((bf16[128,1536]{1,0:T(8,128)(2,1)S(1)}, bf16[128,1536]{1,0:T(8,128)(2,1)S(1)}, u32[]{:S(2)}, u32[]{:S(2)}) %collective-permute-start.21) | collective-permute-done | bytes 393248 | tf_op jit(solution)/shard_map/ppermute | solution.py:924
  353.6 3.0 fusion.21
  356.6 5.2 %collective-permute-done.22 = bf16[64,1536]{1,0:T(8,128)(2,1)S(1)} collective-permute-done((bf16[64,1536]{1,0:T(8,128)(2,1)S(1)}, bf16[64,1536]{1,0:T(8,128)(2,1)S(1)}, u32[]{:S(2)}, u32[]{:S(2)}) %collective-permute-start.22) | collective-permute-done | bytes 196640 | tf_op jit(solution)/shard_map/ppermute | solution.py:924
  (195 shorter events, 90.2 us)
Async XLA Ops:
  7.2 64.7 %all-gather.3.cloned.1.call-start = ((), (), s32[]{:S(2)}) async-start(), calls=%async_computation.1 | async-start | bytes 5849088 | tf_op jit(solution)/shard_map/all_gather | solution.py:981
  11.7 138.3 %all-gather.5.cloned.1.call-start = ((), (), s32[]{:S(2)}) async-start(), calls=%async_computation.2 | async-start | bytes 9191424 | tf_op jit(solution)/shard_map/all_gather | solution.py:983
  13.4 350.9 %reduce-scatter.2.cloned.1.call-start = ((), (), s32[]{:S(2)}) async-start(), calls=%async_computation.3 | async-start | bytes 9191424 | tf_op jit(solution)/shard_map/reduce_scatter | solution.py:1060
  14.1 26.2 %collective-permute-start = (bf16[512,1024]{1,0:T(8,128)(2,1)S(1)}, bf16[512,1024]{1,0:T(8,128)(2,1)S(1)}, u32[]{:S(2)}, u32[]{:S(2)}) collective-permute-start(bf16[512,1024]{1,0:T(8,128)(2,1)S(1)} %fusion.8), channel_id=1, source_target_pairs={{0,1},{1,0},{2,3},{3,2},{4,5},{5,4},{6,7},{7,6},{8,9},{9,8},{10,11... | collective-permute-start | bytes 3145736 | tf_op jit(solution)/shard_map/ppermute | solution.py:833
  40.3 32.9 %collective-permute-start.1 = (bf16[512,1024]{1,0:T(8,128)(2,1)S(1)}, bf16[512,1024]{1,0:T(8,128)(2,1)}, u32[]{:S(2)}, u32[]{:S(2)}) collective-permute-start(bf16[512,1024]{1,0:T(8,128)(2,1)S(1)} %bitcast.72), channel_id=1, source_target_pairs={{0,1},{1,0},{2,3},{3,2},{4,5},{5,4},{6,7},{7,6},{8,9},{9,8},{10,11... | collective-permute-start | bytes 3145736 | tf_op jit(solution)/shard_map/ppermute | solution.py:833
  75.1 35.9 %collective-permute-start.2 = (bf16[1024,512]{1,0:T(8,128)(2,1)S(1)}, bf16[1024,512]{1,0:T(8,128)(2,1)S(1)}, u32[]{:S(2)}, u32[]{:S(2)}) collective-permute-start(bf16[1024,512]{1,0:T(8,128)(2,1)S(1)} %slice.237), channel_id=1, source_target_pairs={{0,1},{1,0},{2,3},{3,2},{4,5},{5,4},{6,7},{7,6},{8,9},{9,8},{10,11... | collective-permute-start | bytes 3145736 | tf_op jit(solution)/shard_map/ppermute | solution.py:833
  112.5 13.9 %collective-permute-start.3 = (bf16[512,512]{1,0:T(8,128)(2,1)S(1)}, bf16[512,512]{1,0:T(8,128)(2,1)S(1)}, u32[]{:S(2)}, u32[]{:S(2)}) collective-permute-start(bf16[512,512]{1,0:T(8,128)(2,1)S(1)} %constant_dynamic-slice_fusion), channel_id=1, source_target_pairs={{0,1},{1,0},{2,3},{3,2},{4,5},{5,4},{6,7},{7,6},{8,9},{9,8},{10,11... | collective-permute-start | bytes 1572872 | tf_op jit(solution)/shard_map/ppermute | solution.py:833
  130.6 15.0 %collective-permute-start.4 = (bf16[256,1024]{1,0:T(8,128)(2,1)S(1)}, bf16[256,1024]{1,0:T(8,128)(2,1)}, u32[]{:S(2)}, u32[]{:S(2)}) collective-permute-start(bf16[256,1024]{1,0:T(8,128)(2,1)S(1)} %get-tuple-element.141), channel_id=1, source_target_pairs={{0,1},{1,0},{2,3},{3,2},{4,5},{5,4},{6,7},{7,6},{8,9},{9,8},{10,11... | collective-permute-start | bytes 1572872 | tf_op jit(solution)/shard_map/ppermute | solution.py:833
  131.1 30.5 %collective-permute-start.6 = (bf16[256,1024]{1,0:T(8,128)(2,1)}, bf16[256,1024]{1,0:T(8,128)(2,1)}, u32[]{:S(2)}, u32[]{:S(2)}) collective-permute-start(bf16[256,1024]{1,0:T(8,128)(2,1)} %get-tuple-element.142), channel_id=1, source_target_pairs={{0,1},{1,0},{2,3},{3,2},{4,5},{5,4},{6,7},{7,6},{8,9},{9,8},{10,11... | collective-permute-start | bytes 1572872 | tf_op jit(solution)/shard_map/ppermute | solution.py:833
  160.1 29.3 %collective-permute-start.5 = (bf16[256,1024]{1,0:T(8,128)(2,1)}, bf16[256,1024]{1,0:T(8,128)(2,1)S(1)}, u32[]{:S(2)}, u32[]{:S(2)}) collective-permute-start(bf16[256,1024]{1,0:T(8,128)(2,1)} %get-tuple-element.66), channel_id=1, source_target_pairs={{0,1},{1,0},{2,3},{3,2},{4,5},{5,4},{6,7},{7,6},{8,9},{9,8},{10,11... | collective-permute-start | bytes 1572872 | tf_op jit(solution)/shard_map/ppermute | solution.py:833
  171.9 17.6 %collective-permute-start.7 = (bf16[256,1024]{1,0:T(8,128)(2,1)}, bf16[256,1024]{1,0:T(8,128)(2,1)S(1)}, u32[]{:S(2)}, u32[]{:S(2)}) collective-permute-start(bf16[256,1024]{1,0:T(8,128)(2,1)} %get-tuple-element.67), channel_id=1, source_target_pairs={{0,1},{1,0},{2,3},{3,2},{4,5},{5,4},{6,7},{7,6},{8,9},{9,8},{10,11... | collective-permute-start | bytes 1572872 | tf_op jit(solution)/shard_map/ppermute | solution.py:833
  196.3 17.2 %collective-permute-start.8 = (bf16[512,512]{1,0:T(8,128)(2,1)}, bf16[512,512]{1,0:T(8,128)(2,1)}, u32[]{:S(2)}, u32[]{:S(2)}) collective-permute-start(bf16[512,512]{1,0:T(8,128)(2,1)} %convolution_convert_fusion), channel_id=1, source_target_pairs={{0,1},{1,0},{2,3},{3,2},{4,5},{5,4},{6,7},{7,6},{8,9},{9,8},{10,11... | collective-permute-start | bytes 1572872 | tf_op jit(solution)/shard_map/ppermute | solution.py:833
  216.9 40.6 %collective-permute-start.10 = (bf16[512,1024]{1,0:T(8,128)(2,1)}, bf16[512,1024]{1,0:T(8,128)(2,1)}, u32[]{:S(2)}, u32[]{:S(2)}) collective-permute-start(bf16[512,1024]{1,0:T(8,128)(2,1)} %copy-done.2), channel_id=1, source_target_pairs={{0,1},{1,0},{2,3},{3,2},{4,5},{5,4},{6,7},{7,6},{8,9},{9,8},{10,11... | collective-permute-start | bytes 3145736 | tf_op jit(solution)/shard_map/ppermute | solution.py:833
  255.1 20.9 %collective-permute-start.11 = (bf16[256,1024]{1,0:T(8,128)(2,1)S(1)}, bf16[256,1024]{1,0:T(8,128)(2,1)}, u32[]{:S(2)}, u32[]{:S(2)}) collective-permute-start(bf16[256,1024]{1,0:T(8,128)(2,1)S(1)} %get-tuple-element.135), channel_id=1, source_target_pairs={{0,1},{1,0},{2,3},{3,2},{4,5},{5,4},{6,7},{7,6},{8,9},{9,8},{10,11... | collective-permute-start | bytes 1572872 | tf_op jit(solution)/shard_map/ppermute | solution.py:833
  276.0 8.7 %collective-permute-start.12 = (bf16[512,1536]{1,0:T(8,128)(2,1)}, bf16[512,1536]{1,0:T(8,128)(2,1)}, u32[]{:S(2)}, u32[]{:S(2)}) collective-permute-start(bf16[512,1536]{1,0:T(8,128)(2,1)} %get-tuple-element.92), channel_id=1, source_target_pairs={{0,2},{2,0},{4,6},{6,4},{8,10},{10,8},{12,14},{14,12},{16,18},{18,... | collective-permute-start | bytes 4718600 | tf_op jit(solution)/shard_map/ppermute | solution.py:924
  276.6 14.1 %collective-permute-start.9 = (bf16[256,1024]{1,0:T(8,128)(2,1)}, bf16[256,1024]{1,0:T(8,128)(2,1)S(1)}, u32[]{:S(2)}, u32[]{:S(2)}) collective-permute-start(bf16[256,1024]{1,0:T(8,128)(2,1)} %get-tuple-element.136), channel_id=1, source_target_pairs={{0,1},{1,0},{2,3},{3,2},{4,5},{5,4},{6,7},{7,6},{8,9},{9,8},{10,11... | collective-permute-start | bytes 1572872 | tf_op jit(solution)/shard_map/ppermute | solution.py:833
  283.7 15.7 %collective-permute-start.23 = (bf16[256,1152]{1,0:T(8,128)(2,1)}, bf16[256,1152]{1,0:T(8,128)(2,1)}, u32[]{:S(2)}, u32[]{:S(2)}) collective-permute-start(bf16[256,1152]{1,0:T(8,128)(2,1)} %add_convert_fusion.2), channel_id=1, source_target_pairs={{0,8},{2,10},{4,12},{6,14},{8,0},{10,2},{12,4},{14,6},{16,24},{18,... | collective-permute-start | bytes 1769480 | tf_op jit(solution)/shard_map/ppermute | solution.py:924
  286.9 22.2 %collective-permute-start.15 = (bf16[256,1536]{1,0:T(8,128)(2,1)}, bf16[256,1536]{1,0:T(8,128)(2,1)}, u32[]{:S(2)}, u32[]{:S(2)}) collective-permute-start(bf16[256,1536]{1,0:T(8,128)(2,1)} %add_convert_fusion.1), channel_id=1, source_target_pairs={{0,4},{2,6},{4,0},{6,2},{8,12},{10,14},{12,8},{14,10},{16,20},{18,... | collective-permute-start | bytes 2359304 | tf_op jit(solution)/shard_map/ppermute | solution.py:924
  300.8 29.1 %collective-permute-start.24 = (bf16[128,1152]{1,0:T(8,128)(2,1)S(1)}, bf16[128,1152]{1,0:T(8,128)(2,1)S(1)}, u32[]{:S(2)}, u32[]{:S(2)}) collective-permute-start(bf16[128,1152]{1,0:T(8,128)(2,1)S(1)} %add_convert_fusion.4), channel_id=1, source_target_pairs={{0,16},{2,18},{4,20},{6,22},{8,24},{10,26},{12,28},{14,30},{16,0},... | collective-permute-start | bytes 884744 | tf_op jit(solution)/shard_map/ppermute | solution.py:924
  310.7 42.9 %collective-permute-start.14 = (bf16[512,1024]{1,0:T(8,128)(2,1)}, bf16[512,1024]{1,0:T(8,128)(2,1)}, u32[]{:S(2)}, u32[]{:S(2)}) collective-permute-start(bf16[512,1024]{1,0:T(8,128)(2,1)} %pad_maximum_fusion.4), channel_id=1, source_target_pairs={{0,1},{1,0},{2,3},{3,2},{4,5},{5,4},{6,7},{7,6},{8,9},{9,8},{10,11... | collective-permute-start | bytes 3145736 | tf_op jit(solution)/shard_map/ppermute | solution.py:833
  312.2 20.0 %collective-permute-start.17 = (f32[18,128]{1,0:T(8,128)S(1)}, f32[18,128]{1,0:T(8,128)S(1)}, u32[]{:S(2)}, u32[]{:S(2)}) collective-permute-start(f32[18,128]{1,0:T(8,128)S(1)} %add.275), channel_id=1, source_target_pairs={{0,4},{2,6},{4,0},{6,2},{8,12},{10,14},{12,8},{14,10},{16,20},{18,... | collective-permute-start | bytes 27656 | tf_op jit(solution)/shard_map/ppermute | solution.py:842
  331.0 6.2 %collective-permute-start.25 = (bf16[64,1152]{1,0:T(8,128)(2,1)S(1)}, bf16[64,1152]{1,0:T(8,128)(2,1)S(1)}, u32[]{:S(2)}, u32[]{:S(2)}) collective-permute-start(bf16[64,1152]{1,0:T(8,128)(2,1)S(1)} %add_convert_fusion.6), channel_id=1, source_target_pairs={{0,4},{2,6},{4,0},{6,2},{8,12},{10,14},{12,8},{14,10},{16,20},{18,... | collective-permute-start | bytes 442376 | tf_op jit(solution)/shard_map/ppermute | solution.py:924
  342.6 8.9 %collective-permute-start.21 = (bf16[128,1536]{1,0:T(8,128)(2,1)S(1)}, bf16[128,1536]{1,0:T(8,128)(2,1)S(1)}, u32[]{:S(2)}, u32[]{:S(2)}) collective-permute-start(bf16[128,1536]{1,0:T(8,128)(2,1)S(1)} %add_convert_fusion.3), channel_id=1, source_target_pairs={{0,8},{2,10},{4,12},{6,14},{8,0},{10,2},{12,4},{14,6},{16,24},{18,... | collective-permute-start | bytes 1179656 | tf_op jit(solution)/shard_map/ppermute | solution.py:924
  352.8 8.9 %collective-permute-start.22 = (bf16[64,1536]{1,0:T(8,128)(2,1)S(1)}, bf16[64,1536]{1,0:T(8,128)(2,1)S(1)}, u32[]{:S(2)}, u32[]{:S(2)}) collective-permute-start(bf16[64,1536]{1,0:T(8,128)(2,1)S(1)} %add_convert_fusion.5), channel_id=1, source_target_pairs={{0,16},{2,18},{4,20},{6,22},{8,24},{10,26},{12,28},{14,30},{16,0},... | collective-permute-start | bytes 589832 | tf_op jit(solution)/shard_map/ppermute | solution.py:924
  (28 other events, 283.2 us)
Sparse Core Ops, SparseCore 0:
  11.8 60.0 all-gather.2
  74.8 75.1 all-gather.4
  217.0 117.6 reduce-scatter.1
where the time goes:
time: 383 us; the launch traced here: 378 us
  Pallas kernels  128 us (33%)
  waiting for transfers between devices  125 us (33%)
  other arithmetic  33 us (9%)
  local copies, waits for them, and re-layouts  30.8 us (8%)
  starting transfers between devices  25.3 us (7%)
  matrix products  21.6 us (6%)
  between operations  14.7 us (4%)
    ppermute x13, waiting for transfers between devices, swap(): return lax.ppermute(rows, 'tensor', [(0, 1), (1, 0)])  51 us
    ppermute x8, waiting for transfers between devices, flip(): return lax.ppermute(values, 'dp', [(i, i ^ 1 << bit) for i in range(size)])  39.8 us
    pallas_call x3, Pallas kernels, ffn(): pl.pallas_call(functools.partial(ffn_kernel, tiles), grid=(len(tiles),),...  35.2 us
    pallas_call x1, Pallas kernels, mixer_backward(): pl.pallas_call(functools.partial(backward_kernel, heads), grid=(count,),...  28.1 us
    all_gather x1, waiting for transfers between devices, local(): mix_full = lax.all_gather(mixer_pack, 'dp', axis=0, tiled=True)  27.2 us
    pallas_call x1, Pallas kernels, mixer_forward(): pl.pallas_call(functools.partial(forward_kernel, heads, subs), grid=(coun...  20.8 us
    dot_general x4, matrix products, contract_last(): lax.dot_general(operand, other, (((1,), (1,)), ((), ())), preferred_eleme...  17.7 us
    ppermute x13, starting transfers between devices, swap(): return lax.ppermute(rows, 'tensor', [(0, 1), (1, 0)])  16.7 us
  transfers between devices with their start and end apart: 29, of which 14 were waited for; matrix products, arithmetic and copies ran while one was open for 17% of the time, Pallas kernels for 34%

commit v1 on v0

--- a/solution.py
+++ b/solution.py
@@ -140,18 +140,32 @@
 
 
 def forward_kernel(
-    heads, subs, proj_ref, seg_ref, conv_ref, rate_ref, gain_ref,
-    mixed_ref, inverse_ref, w_ref, pseudo_ref, out_ref, state_ref, conv_out_ref,
-    state, halo, seg_halo,
+    heads, subs, x_ref, weight_ref, seg_ref, conv_ref, rate_ref, gain_ref,
+    proj_ref, mixed_ref, inverse_ref, w_ref, pseudo_ref, out_ref, state_ref, conv_out_ref,
+    state, halo, seg_halo, ahead,
 ):
     step = pl.program_id(0)
+    block_rows = subs * CHUNK
+    width = proj_ref.shape[1]
+
+    def project(block, lanes):
+        rows = x_ref[pl.ds(pl.multiple_of(block * block_rows, block_rows), block_rows), :]
+        ahead[:, lanes] = dot(rows, weight_ref[:, lanes], NN)
+
+    column_tiles = [
+        slice(at, min(at + COLUMN_TILE, width)) for at in range(0, width, COLUMN_TILE)
+    ]
 
     @pl.when(step == 0)
     def _():
         state[...] = jnp.zeros_like(state)
         halo[...] = jnp.zeros_like(halo)
         seg_halo[...] = jnp.full_like(seg_halo, -1.0)
-
+        for lanes in column_tiles:
+            project(0, lanes)
+
+    proj_ref[...] = ahead[...]
+    following = jnp.minimum(step + 1, pl.num_programs(0) - 1)
     row, col = grids()
     wide = heads * WIDTH
     each = range(heads)
@@ -227,6 +241,9 @@
         for work in (query_of, target_of, scores_of, gate_of)
         for item in items
     ]
+    for at, lanes in enumerate(column_tiles):
+        place = at * (len(beside) // len(column_tiles) + 1)
+        beside.insert(place, functools.partial(project, following, lanes))
     inverses = unit_lower_inverses(lowers, row, col, beside)
     inverses = {item: inverse.astype(bf16) for item, inverse in zip(items, inverses)}
     halo[...] = proj_ref[subs * CHUNK - HALO :, : 3 * wide]
@@ -266,8 +283,19 @@
 
 
 def backward_kernel(
-    heads, proj_ref, seg_ref, seg_before_ref, before_ref, conv_ref, rate_ref, gain_ref, grad_ref,
-    inverse_ref, w_ref, pseudo_ref, out_ref, state_ref, conv_out_ref,
+    heads, parts, rank_ref, proj_ref, seg_ref, seg_before_ref, before_ref, conv_ref, rate_ref,
+    gain_ref, *refs
+):
+    grad_refs, refs = refs[:parts], refs[parts:]
+    backward_steps(
+        heads, rank_ref, proj_ref, seg_ref, seg_before_ref, before_ref, conv_ref, rate_ref,
+        gain_ref, grad_refs, *refs
+    )
+
+
+def backward_steps(
+    heads, rank_ref, proj_ref, seg_ref, seg_before_ref, before_ref, conv_ref, rate_ref, gain_ref,
+    grad_refs, inverse_ref, w_ref, pseudo_ref, out_ref, state_ref, conv_out_ref,
     dproj_ref, dconv_ref, drate_ref, dgain_ref,
     dstate, carry_halo,
 ):
@@ -359,13 +387,17 @@
         for h in each
     ]
 
+    half = pl.num_programs(0) // 2
+    from_own = (pl.num_programs(0) - 1 - step) // half == rank_ref[0]
     dout = []
     for head, lanes in enumerate(head_lanes):
         gate_at = slice(3 * wide + head * WIDTH, 3 * wide + (head + 1) * WIDTH)
         gate = proj_ref[:, gate_at]
         gate_s = sigmoid(gate)
         gate_act = gate * gate_s
-        grad = grad_ref[:, lanes].astype(f32)
+        grad = grad_refs[0][:, lanes].astype(f32)
+        if len(grad_refs) == 2:
+            grad = jnp.where(from_own, grad, grad_refs[1][:, lanes].astype(f32))
         output = out_ref[:, lanes]
         inv_rms = lax.rsqrt(jnp.mean(output * output, axis=-1, keepdims=True) + norm_eps)
         unit = output * inv_rms
@@ -470,10 +502,10 @@
     ).astype(bf16)
 
 
-def mixer_forward(proj, seg_wide, conv_rows, neg_rate, gain):
-    length, width = proj.shape
-    heads = (width - WIDTH) // (4 * WIDTH)
+def mixer_forward(x, weights, heads, seg_wide, conv_rows, neg_rate, gain):
+    length, model = x.shape
     wide = heads * WIDTH
+    width = 4 * wide + WIDTH
     count = length // CHUNK
     subs = 2 if count % 2 == 0 else 1
     by_chunk = lambda cols: pl.BlockSpec((subs * CHUNK, cols), lambda i: (i, 0))
@@ -482,14 +514,15 @@
         functools.partial(forward_kernel, heads, subs),
         grid=(count // subs,),
         in_specs=[
-            by_chunk(width), by_chunk(WIDTH), whole(12, wide), whole(1, WIDTH), whole(1, WIDTH),
+            whole(length, model), whole(model, width), by_chunk(WIDTH), whole(12, wide), whole(1, WIDTH), whole(1, WIDTH),
         ],
         out_specs=[
-            by_chunk(wide), by_chunk(wide), by_chunk(wide), by_chunk(wide), by_chunk(wide),
+            by_chunk(width), by_chunk(wide), by_chunk(wide), by_chunk(wide), by_chunk(wide), by_chunk(wide),
             pl.BlockSpec((subs, heads, WIDTH, WIDTH), lambda i: (i, 0, 0, 0)),
             by_chunk(3 * wide),
         ],
         out_shape=[
+            pltpu.HBM((length, width), f32),
             pltpu.HBM((length, wide), bf16),
             pltpu.HBM((length, wide), bf16),
             pltpu.HBM((length, wide), bf16),
@@ -502,48 +535,64 @@
             pltpu.VMEM((heads, WIDTH, WIDTH), f32),
             pltpu.VMEM((HALO, 3 * wide), f32),
             pltpu.VMEM((HALO, WIDTH), f32),
+            pltpu.VMEM((subs * CHUNK, width), f32),
         ],
         compiler_params=pltpu.CompilerParams(vmem_limit_bytes=48 * 1024 * 1024),
         cost_estimate=pl.CostEstimate(
-            flops=2 * 160 * length * WIDTH * wide,
-            bytes_accessed=4 * length * (width + 3 * wide),
+            flops=2 * 160 * length * WIDTH * wide + 2 * length * model * width,
+            bytes_accessed=2 * model * (length + width) + 4 * length * (width + 6 * wide),
             transcendentals=8 * length * wide,
         ),
         name="mixer_forward",
-    )(*in_hbm(proj, seg_wide, conv_rows, neg_rate, gain))
-
-
-def mixer_backward(proj, seg_wide, conv_rows, neg_rate, gain, grad, saved):
+    )(*in_hbm(x, weights, seg_wide, conv_rows, neg_rate, gain))
+
+
+def mixer_backward(proj, seg_wide, conv_rows, neg_rate, gain, rank, grads, saved):
     length, width = proj.shape
     heads = (width - WIDTH) // (4 * WIDTH)
     wide = heads * WIDTH
     count = length // CHUNK
     back = lambda i: count - 1 - i
-    by_chunk = lambda cols: pl.BlockSpec((CHUNK, cols), lambda i: (back(i), 0))
+    by_chunk = lambda cols: pl.BlockSpec((CHUNK, cols), lambda i, rank: (back(i), 0))
     before = lambda cols: pl.BlockSpec(
-        (HALO, cols), lambda i: (jnp.maximum(back(i) * (CHUNK // HALO) - 1, 0), 0)
-    )
-    whole = lambda rows, cols: pl.BlockSpec((rows, cols), lambda i: (0, 0))
-    return pl.pallas_call(
-        functools.partial(backward_kernel, heads),
+        (HALO, cols), lambda i, rank: (jnp.maximum(back(i) * (CHUNK // HALO) - 1, 0), 0)
+    )
+    whole = lambda rows, cols: pl.BlockSpec((rows, cols), lambda i, rank: (0, 0))
+    part_count = grads[0].shape[0] // CHUNK
+
+    def grad_block(other):
+        def index(i, rank):
+            first = (1 - rank[0] if other else rank[0]) * part_count
+            return jnp.clip(back(i) - first, 0, part_count - 1), 0
+
+        return pl.BlockSpec((CHUNK, wide), index)
+
+    grad_blocks = [grad_block(False), grad_block(True)] if len(grads) == 2 else [by_chunk(wide)]
+    grid_spec = pltpu.PrefetchScalarGridSpec(
+        num_scalar_prefetch=1,
         grid=(count,),
         in_specs=[
             by_chunk(width), by_chunk(WIDTH), before(WIDTH), before(3 * wide),
             whole(12, wide), whole(1, WIDTH), whole(1, WIDTH),
-            by_chunk(wide), by_chunk(wide), by_chunk(wide), by_chunk(wide), by_chunk(wide),
-            pl.BlockSpec((1, heads, WIDTH, WIDTH), lambda i: (back(i), 0, 0, 0)),
+            *grad_blocks,
+            by_chunk(wide), by_chunk(wide), by_chunk(wide), by_chunk(wide),
+            pl.BlockSpec((1, heads, WIDTH, WIDTH), lambda i, rank: (back(i), 0, 0, 0)),
             by_chunk(3 * wide),
         ],
         out_specs=[by_chunk(width), whole(12, wide), whole(1, WIDTH), whole(1, WIDTH)],
+        scratch_shapes=[
+            pltpu.VMEM((heads, WIDTH, WIDTH), f32),
+            pltpu.VMEM((HALO, 3 * wide), f32),
+        ],
+    )
+    return pl.pallas_call(
+        functools.partial(backward_kernel, heads, len(grads)),
+        grid_spec=grid_spec,
         out_shape=[
             pltpu.HBM((length, width), bf16),
             pltpu.HBM((12, wide), f32),
             pltpu.HBM((1, WIDTH), f32),
             pltpu.HBM((1, WIDTH), f32),
-        ],
-        scratch_shapes=[
-            pltpu.VMEM((heads, WIDTH, WIDTH), f32),
-            pltpu.VMEM((HALO, 3 * wide), f32),
         ],
         compiler_params=pltpu.CompilerParams(vmem_limit_bytes=48 * 1024 * 1024),
         cost_estimate=pl.CostEstimate(
@@ -552,32 +601,7 @@
             transcendentals=8 * length * wide,
         ),
         name="mixer_backward",
-    )(*in_hbm(proj, seg_wide, seg_wide, proj, conv_rows, neg_rate, gain, grad, *saved))
-
-
-def project_kernel(x_ref, w_ref, out_ref):
-    out_ref[...] = dot(x_ref[...], w_ref[...], NN)
-
-
-def project(x, packed, columns):
-    rows, model = x.shape
-    return pl.pallas_call(
-        project_kernel,
-        grid=(pl.cdiv(columns, COLUMN_TILE),),
-        in_specs=[
-            pl.BlockSpec((rows, model), lambda i: (0, 0)),
-            pl.BlockSpec((model, COLUMN_TILE), lambda i: (0, i)),
-        ],
-        out_specs=pl.BlockSpec((rows, COLUMN_TILE), lambda i: (0, i)),
-        out_shape=pltpu.HBM((rows, columns), f32),
-        compiler_params=pltpu.CompilerParams(vmem_limit_bytes=40 * 1024 * 1024),
-        cost_estimate=pl.CostEstimate(
-            flops=2 * rows * model * columns,
-            bytes_accessed=2 * model * (rows + columns) + 4 * rows * columns,
-            transcendentals=0,
-        ),
-        name="project",
-    )(*in_hbm(x, packed))
+    )(rank, *in_hbm(proj, seg_wide, seg_wide, proj, conv_rows, neg_rate, gain, *grads, *saved))
 
 
 def ffn_kernel(tiles, x_ref, dy_ref, w_ref, h_ref, g_ref, y_ref, dx_ref, y_sum, dx_sum):
@@ -653,6 +677,16 @@
     )(*in_hbm(x, dy, packed))
 
 
+def turn_rows(core_ref, order, turned, source):
+    half = len(order) // 2
+    size = source.shape[0] // len(order)
+    for at, block in enumerate(order):
+        away = (block % 2 + 1 + core_ref[0]) % 2
+        begin = (away * half + at % half) * size
+        rows = pl.ds(pl.multiple_of(begin, size), size)
+        turned[rows, :] = source[block * size : (block + 1) * size, :]
+
+
 def ffn_grads_kernel(tiles, *refs):
     *inputs, out_ref, x_turned, dy_turned = refs
     count = len(inputs) // 4
@@ -705,11 +739,22 @@
     )(*in_hbm(*xs, *dys, *hs, *gs))
 
 
+def turn_rows(core_ref, order, turned, source):
+    half = len(order) // 2
+    size = source.shape[0] // len(order)
+    for at, block in enumerate(order):
+        away = (block % 2 + 1 + core_ref[0]) % 2
+        begin = (away * half + at % half) * size
+        rows = pl.ds(pl.multiple_of(begin, size), size)
+        turned[rows, :] = source[block * size : (block + 1) * size, :]
+
+
 def mixer_grads_kernel(
-    orders, split, main_steps, core_ref, normed_ref, residual_ref, dproj_ref, mixed_ref, conv_ref,
-    first_sent_ref, first_kept_ref, second_sent_ref, second_kept_ref,
-    turned, residual_turned, conv_turned,
+    orders, split, main_steps, parts, core_ref, normed_ref, dproj_ref, conv_ref, *refs
 ):
+    residual_refs, mixed_refs, refs = refs[:parts], refs[parts : 2 * parts], refs[2 * parts :]
+    first_sent_ref, first_kept_ref, second_sent_ref, second_kept_ref, *refs = refs
+    turned, conv_turned, *residuals_turned = refs
     step = pl.program_id(0)
     last = pl.num_programs(0) - 1
     first_order, second_order = orders
@@ -718,16 +763,10 @@
 
     @pl.when(step == 0)
     def _():
-        normed = normed_ref[...].T
-        residual = residual_ref[...].T
-        for at, block in enumerate(first_order):
-            away = (block % 2 + 1 + core_ref[0]) % 2
-            begin = (away * (count // 2) + at % (count // 2)) * size
-            rows = pl.ds(pl.multiple_of(begin, size), size)
-            from_rows = slice(block * size, (block + 1) * size)
-            turned[rows, :] = normed[from_rows]
-            residual_turned[rows, :] = residual[from_rows]
-            conv_turned[rows, :] = conv_ref[from_rows, :]
+        turn_rows(core_ref, first_order, turned, normed_ref[...].T)
+        for residual_turned, residual_ref in zip(residuals_turned, residual_refs):
+            turn_rows(core_ref, first_order, residual_turned, residual_ref[...].T)
+        turn_rows(core_ref, first_order, conv_turned, conv_ref[...])
 
     def store(grads, lanes):
         grads = grads.astype(bf16)
@@ -752,47 +791,53 @@
 
     @pl.when((step >= main_steps) & (step < last))
     def _():
-        store(dot(residual_turned[...], mixed_ref[...], NN), slice(None))
+        grads = 0.0
+        for residual_turned, mixed_ref in zip(residuals_turned, mixed_refs):
+            grads = grads + dot(residual_turned[...], mixed_ref[...], NN)
+        store(grads, slice(None))
 
     @pl.when(step == last)
     def _():
         store(dot(turned[...], dproj_ref[:, :WIDTH], NN) + conv_turned[...], slice(0, WIDTH))
 
 
-def mixer_grads(normed, residual, dproj, mixed, conv_block, core, orders):
+def mixer_grads(normed, residuals, dproj, mixed_parts, conv_block, core, orders):
     rows, model = normed.shape
-    wide = mixed.shape[1]
+    wide = mixed_parts[0].shape[1]
+    parts = len(residuals)
+    part_rows = residuals[0].shape[0]
     tile = 2 * WIDTH if wide % (2 * WIDTH) == 0 else WIDTH
     main_steps = 4 * wide // tile
     out_steps = wide // tile
     columns = 5 * wide + WIDTH
-    split = (main_steps + out_steps + 1) * 5 // 9
+    split = (main_steps + out_steps + 1) * 5 // 11
     first = split * tile
-    whole = lambda cols: pl.BlockSpec((rows, cols), lambda i, core: (0, 0))
+    whole = lambda rows, cols: pl.BlockSpec((rows, cols), lambda i, core: (0, 0))
+    mixed_block = pl.BlockSpec(
+        (part_rows, tile), lambda i, core: (0, jnp.clip(i - main_steps, 0, out_steps - 1))
+    )
     first_block = pl.BlockSpec((model // 2, tile), lambda i, core: (0, jnp.minimum(i, split - 1)))
     second_block = pl.BlockSpec((model // 2, tile), lambda i, core: (0, jnp.maximum(i - split, 0)))
     first_shape = pltpu.HBM((model // 2, first), bf16)
     second_shape = pltpu.HBM((model // 2, columns - first), bf16)
     return pl.pallas_call(
-        functools.partial(mixer_grads_kernel, orders, split, main_steps),
+        functools.partial(mixer_grads_kernel, orders, split, main_steps, parts),
         grid_spec=pltpu.PrefetchScalarGridSpec(
             num_scalar_prefetch=1,
             grid=(main_steps + out_steps + 1,),
             in_specs=[
-                whole(model),
-                whole(model),
+                whole(rows, model),
                 pl.BlockSpec((rows, tile), lambda i, core: (0, jnp.minimum(i, main_steps))),
-                pl.BlockSpec(
-                    (rows, tile), lambda i, core: (0, jnp.clip(i - main_steps, 0, out_steps - 1))
-                ),
-                pl.BlockSpec((model, WIDTH), lambda i, core: (0, 0)),
-            ],
+                whole(model, WIDTH),
+            ]
+            + [whole(part_rows, model)] * parts
+            + [mixed_block] * parts,
             out_specs=[first_block, first_block, second_block, second_block],
             scratch_shapes=[
                 pltpu.VMEM((model, rows), bf16),
-                pltpu.VMEM((model, rows), bf16),
                 pltpu.VMEM((model, WIDTH), f32),
-            ],
+            ]
+            + [pltpu.VMEM((model, part_rows), bf16)] * parts,
         ),
         out_shape=[first_shape, first_shape, second_shape, second_shape],
         compiler_params=pltpu.CompilerParams(vmem_limit_bytes=40 * 1024 * 1024),
@@ -802,7 +847,7 @@
             transcendentals=0,
         ),
         name="mixer_grads",
-    )(core, *in_hbm(normed, residual, dproj, mixed, conv_block))
+    )(core, *in_hbm(normed, dproj, conv_block, *residuals, *mixed_parts))
 
 
 def rms_norm(values, scales):
@@ -833,34 +878,40 @@
     return lax.ppermute(rows, "tensor", [(0, 1), (1, 0)])
 
 
-def sum_over(values, axis):
+def sum_steps(axis):
     size = lax.axis_size(axis)
     if size & (size - 1):
-        return lax.psum(values, axis)
-    bit = 1
-    while bit < size:
-        values = values + lax.ppermute(values, axis, [(i, i ^ bit) for i in range(size)])
-        bit *= 2
-    return values
+        return [lambda values: lax.psum(values, axis)]
+
+    def step(bit, values):
+        def across(mask):
+            return lax.ppermute(values, axis, [(i, i ^ mask) for i in range(size)])
+
+        if 2 * bit < size:
+            return (values + across(bit)) + (across(2 * bit) + across(3 * bit))
+        return values + across(bit)
+
+    return [functools.partial(step, 1 << at) for at in range(0, size.bit_length() - 1, 2)]
 
 
 def hidden_tiles(hidden):
     if hidden % WIDTH:
         return (hidden,)
-    return (2 * WIDTH,) * (hidden // (2 * WIDTH)) + (WIDTH,) * (hidden // WIDTH % 2)
-
-
-def pack_tiles(gate, up, down, tiles):
+    size = min(4 * WIDTH, hidden)
+    return (size,) * (hidden // size) + ((hidden % size,) if hidden % size else ())
+
+
+def pack_tiles(parts, tiles):
     blocks = []
     at = 0
     for size in tiles:
-        blocks += [part[:, at : at + size] for part in (gate, up, down)]
+        blocks += [part[:, at : at + size] for part in parts]
         at += size
     return jnp.concatenate(blocks, axis=1)
 
 
-def unpack_tiles(packed, tiles):
-    parts = ([], [], [])
+def unpack_tiles(packed, tiles, count):
+    parts = [[] for _ in range(count)]
     at = 0
     for size in tiles:
         for part in parts:
@@ -870,7 +921,7 @@
 
 
 def ffn_plain(x, dy, packed, tiles):
-    gate_w, up_w, down_w = unpack_tiles(packed, tiles)
+    gate_w, up_w, down_w = unpack_tiles(packed, tiles, 3)
     gate = jnp.dot(x, gate_w, preferred_element_type=f32)
     up = jnp.dot(x, up_w, preferred_element_type=f32)
     grad = jnp.dot(dy, down_w, preferred_element_type=f32)
@@ -886,12 +937,12 @@
 
 def ffn_grads_plain(x, dy, hidden, grads, tiles):
     size = hidden.shape[1]
-    return pack_tiles(
-        contract_first(x, grads[:, :size]).astype(bf16),
-        contract_first(x, grads[:, size:]).astype(bf16),
-        contract_first(dy, hidden).astype(bf16),
-        tiles,
-    )
+    parts = [
+        contract_first(x, grads[:, :size]),
+        contract_first(x, grads[:, size:]),
+        contract_first(dy, hidden),
+    ]
+    return pack_tiles([part.astype(bf16) for part in parts], tiles)
 
 
 def bit_orders(size):
@@ -979,7 +1030,7 @@
         axis=1,
     )
     mix_full = lax.all_gather(mixer_pack, "dp", axis=0, tiled=True)
-    ffn_pack = pack_tiles(w_gate_up[:, 0], w_gate_up[:, 1], w_down.T, tiles)
+    ffn_pack = pack_tiles([w_gate_up[:, 0], w_gate_up[:, 1], w_down.T], tiles)
     ffn_full = lax.all_gather(ffn_pack, "dp", axis=0, tiled=True)
     out_mine = mix_full[:, projected_width:]
     conv_at = 4 * wide + 2 * heads
@@ -1002,7 +1053,9 @@
     normed = normed.astype(bf16)
     if pair:
         normed_other = swap(normed)
-        grad_sent, normed_other = lax.optimization_barrier((grad_own, normed_other))
+        grad_sent, normed_other, segment, neg_rate = lax.optimization_barrier(
+            (grad_own, normed_other, segment, neg_rate)
+        )
         grad_other = swap(grad_sent)
         normed_all, grad_other, out_sent = lax.optimization_barrier(
             (in_order(normed, normed_other), grad_other, out_mine)
@@ -1010,8 +1063,9 @@
         out_other = swap(out_sent)
     else:
         normed_all = gather_rows(normed)
-    projected = project(normed_all, mix_full, projected_width)
-    mixed, *saved = mixer_forward(projected, segment, conv_rows, neg_rate, gain_row)
+    projected, mixed, *saved = mixer_forward(
+        normed_all, mix_full, heads, segment, conv_rows, neg_rate, gain_row
+    )
     if pair:
         mixed, out_other = lax.optimization_barrier((mixed, out_other))
         mixed_own, mixed_theirs = own_and_other(mixed)
@@ -1039,6 +1093,9 @@
         done = [one_ffn(x_parts[0], dy_parts[0], ffn_full, tiles)]
         dx = scatter_rows(done[0][3]).astype(f32)
     h_parts, g_parts, y_parts, _ = zip(*done)
+    core = lax.axis_index("dp") % 2
+    bits = bit_orders(dp_size)
+    orders = [block_order(dp_size, order) for order in bits]
     if kernels:
         ffn_sums = ffn_grads(x_parts, dy_parts, h_parts, g_parts, tiles)
     else:
@@ -1049,101 +1106,109 @@
     if pair:
         grad_theirs = jnp.dot(residual_low, out_other, preferred_element_type=f32).astype(bf16)
         grad_mine = jnp.dot(residual_low, out_mine, preferred_element_type=f32).astype(bf16)
-        mixed_grad = in_order(grad_mine, swap(grad_theirs))
-        mixed_grad, ffn_sums, residual_sent, y_sent = lax.optimization_barrier(
-            (mixed_grad, ffn_sums, residual_low, jnp.concatenate(y_parts[1:], axis=0))
+        grad_mine, mixed_grad, ffn_sums, residual_sent, y_first, y_last = lax.optimization_barrier(
+            (
+                grad_mine,
+                swap(grad_theirs),
+                ffn_sums,
+                residual_low,
+                y_parts[1],
+                y_parts[2],
+            )
         )
-        residual_all = in_order(residual_low, swap(residual_sent))
+        mixed_grads = [grad_mine, mixed_grad]
+        residuals = [residual_low, swap(residual_sent)]
+        mixed_parts = [mixed_own, mixed_theirs]
     else:
-        residual_all = gather_rows(residual_low)
-        mixed_grad = jnp.dot(residual_all, out_mine, preferred_element_type=f32).astype(bf16)
+        residuals = [gather_rows(residual_low)]
+        mixed_grads = [jnp.dot(residuals[0], out_mine, preferred_element_type=f32).astype(bf16)]
+        mixed_parts = [mixed]
     ffn_owned = lax.psum_scatter(ffn_sums, "dp", scatter_dimension=0, tiled=True)
     projection_grad, conv_grad, log_grad, gain_grad = mixer_backward(
-        projected, segment, conv_rows, neg_rate, gain_row, mixed_grad, saved
+        projected, segment, conv_rows, neg_rate, gain_row, tensor_rank[None], mixed_grads, saved
     )
     conv_grad = jnp.pad(
         conv_grad.reshape(12 * heads, WIDTH).T.reshape(dp_size, taps_here, 12 * heads),
         ((0, 0), (0, rows_here - taps_here), (2 * heads, WIDTH - 14 * heads)),
     ).reshape(model_width, WIDTH)
-    core = lax.axis_index("dp") % 2
-    bits = bit_orders(dp_size)
-    orders = [block_order(dp_size, order) for order in bits]
     mix_rows = mix_full[:, :projected_width]
-    if pair:
-        grad_here, grad_there = own_and_other(projection_grad)
-        sent = contract_last(grad_there, mix_rows).astype(bf16)
-        sent, projection_grad = lax.optimization_barrier((sent, projection_grad))
-        half = own_rows // 2
-        received, received_late = swap(sent[:half]), swap(sent[half:])
-    else:
-        received = scatter_rows(contract_last(projection_grad, mix_rows))
     first_sent, first_kept, second_sent, second_kept = mixer_grads(
-        normed_all, residual_all, projection_grad, mixed, conv_grad, core[None], orders
-    )
-    if pair:
-        first_sent, second_sent, received = lax.optimization_barrier(
-            (first_sent, second_sent, received)
-        )
+        normed_all, residuals, projection_grad, mixed_parts, conv_grad, core[None], orders
+    )
+    projection_grad, _, _ = lax.optimization_barrier((projection_grad, first_sent, second_sent))
     second = [second_kept, flip(second_sent, 0)]
     first = [first_kept, flip(first_sent, 0)]
     second_out = outgoing(second, bits[1][1])
     first_out = outgoing(first, bits[0][1])
     if pair:
-        received_late, y_sent, _, _ = lax.optimization_barrier(
-            (received_late, y_sent, first_out, second_out)
-        )
-        received = jnp.concatenate([received, received_late], axis=0)
-        y_other = swap(y_sent)
+        grad_here, grad_there = own_and_other(projection_grad)
+        sent = contract_last(grad_there, mix_rows).astype(bf16)
+        first_out, second_out, sent = lax.optimization_barrier((first_out, second_out, sent))
+        received = swap(sent)
+    else:
+        received = scatter_rows(contract_last(projection_grad, mix_rows))
+    first = settle(first, bits[0][1], first_out)
+    second = settle(second, bits[1][1], second_out)
+    first_out = outgoing(first, bits[0][2])
+    second_out = outgoing(second, bits[1][2])
+    if pair:
+        y_first, y_last, _ = lax.optimization_barrier((y_first, y_last, second_out))
+        received, grad_here, _ = lax.optimization_barrier((received, grad_here, first_out))
+        y_other = jnp.concatenate([swap(y_first), swap(y_last)], axis=0)
+        mixer_input_grad = received.astype(f32) + contract_last(grad_here, mix_rows)
     else:
         y_other = scatter_rows(y_parts[0])
-    second = settle(second, bits[1][1], second_out)
-    first = settle(first, bits[0][1], first_out)
-    mixer_input_grad = received.astype(f32)
-    y = y_other.astype(f32)
-    if pair:
-        mixer_input_grad = mixer_input_grad + contract_last(grad_here, mix_rows)
-        y = y + y_parts[0].astype(f32)
-    out_tokens = (residual + y).astype(bf16)[None]
+        mixer_input_grad = received.astype(f32)
+    first = settle(first, bits[0][2], first_out)
+    second = settle(second, bits[1][2], second_out)
     input_part, first_gains = first_back(mixer_input_grad)
     input_grad = (residual_grad + input_part).astype(bf16)[None]
     log_full = lax.dynamic_update_slice_in_dim(
         jnp.zeros(a_log.shape, f32), log_grad[0, :heads], tensor_rank * heads, 0
     )
-    small = jnp.concatenate(
-        [
-            (first_gains + second_gains).reshape(-1, WIDTH),
-            gain_grad,
-            jnp.pad(log_full, (0, WIDTH - log_full.shape[0]))[None],
-        ]
-    )
-    for one, other in zip(bits[0][2:], bits[1][2:]):
+    last_row = jnp.concatenate([gain_grad[0], log_full])
+    last_row = jnp.pad(last_row, (0, model_width - last_row.shape[0]))[None]
+    small = jnp.concatenate([first_gains + second_gains, last_row], axis=0)
+    for one, other in zip(bits[0][3:], bits[1][3:]):
+        last_out = first_out
+        first_out = outgoing(first, one)
         second_out = outgoing(second, other)
-        first_out = outgoing(first, one)
-        if one == bits[0][2]:
-            small, _ = lax.optimization_barrier((small, first_out))
+        second_out, _ = lax.optimization_barrier((second_out, last_out))
+        small, _ = lax.optimization_barrier((small, first_out))
+        first = settle(first, one, first_out)
         second = settle(second, other, second_out)
-        first = settle(first, one, first_out)
+    y = y_other.astype(f32)
+    if pair:
+        y = y + y_parts[0].astype(f32)
+    out_tokens = (residual + y).astype(bf16)[None]
+    *steps, last_step = sum_steps("tensor") + sum_steps("dp")
+    for step in steps:
+        small = step(small)
+    gate_grad, up_grad, down_grad = unpack_tiles(ffn_owned, tiles, 3)
+    up_owned = jnp.stack([gate_grad, up_grad], axis=1).astype(f32)
+    down_owned = down_grad.T.astype(f32)
+    small = last_step(small)
+    first[-1], out_tokens, up_owned, down_owned = lax.optimization_barrier(
+        (first[-1], out_tokens, up_owned, down_owned)
+    )
     mix_owned = jnp.concatenate(
         [sum(term.astype(f32) for term in terms) for terms in (first, second)], axis=1
     )
-    small = sum_over(sum_over(small, "dp"), "tensor")
-    gain_rows = 2 * model_width // WIDTH
-    gate_grad, up_grad, down_grad = unpack_tiles(ffn_owned, tiles)
     rates = mix_owned[:, 5 * wide :]
     return (
         out_tokens,
         input_grad,
-        small[:gain_rows].reshape(2, model_width),
+        small[:2],
         mix_owned[:, : 4 * wide].reshape(w_mixer_in.shape),
         rates[:, : 2 * heads].reshape(w_rates.shape),
         rates[:taps_here, 2 * heads : 14 * heads]
         .reshape(taps_here, 3, 4, heads)
         .transpose(1, 2, 3, 0),
-        small[gain_rows + 1, : a_log.shape[0]],
-        small[gain_rows],
+        small[2, WIDTH : WIDTH + a_log.shape[0]],
+        small[2, :WIDTH],
         mix_owned[:, 4 * wide : 5 * wide].T,
-        jnp.stack([gate_grad, up_grad], axis=1).astype(f32),
-        down_grad.T.astype(f32),
+        up_owned,
+        down_owned,
     )
 
 

time: 383 us -> 368 us (0.961)
  other arithmetic: 33 us -> 24.8 us
  starting transfers between devices: 25.3 us -> 33.1 us
  Pallas kernels: 128 us -> 121 us
    pallas_call x2 -> x1, Pallas kernels: 40.8 us -> 28.2 us  [mixer_backward(): pl.pallas_call(functools.partial(backward_kernel, heads, len(grads)), gri...]
    ppermute x5 -> x7, starting transfers between devices: 1.76 us -> 9.32 us  [across(): return lax.ppermute(values, axis, [(i, i ^ mask) for i in range(size)])]
    pallas_call x1, Pallas kernels: 20.8 us -> 28.1 us  [mixer_forward(): pl.pallas_call(functools.partial(forward_kernel, heads, subs), grid=(coun...]
    all_gather x1, waiting for transfers between devices: 4.36 us -> 10.7 us  [local(): ffn_full = lax.all_gather(ffn_pack, 'dp', axis=0, tiled=True)]
    unnamed x69 -> x59, local copies, waits for them, and re-layouts: 7.4 us -> 2.38 us
  transfers between devices with their start and end apart: 29 -> 31, of which waited for: 14 -> 10; matrix products, arithmetic and copies ran while one was open for 17% -> 15% of each run, Pallas kernels for 34% -> 33%
where the time goes in v1:
time: 368 us; the launch traced here: 364 us
  waiting for transfers between devices  124 us (34%)
  Pallas kernels  121 us (33%)
  starting transfers between devices  33.1 us (9%)
  local copies, waits for them, and re-layouts  27.2 us (7%)
  other arithmetic  24.8 us (7%)
  matrix products  19.3 us (5%)
  between operations  14.6 us (4%)
    ppermute x13, waiting for transfers between devices, swap(): return lax.ppermute(rows, 'tensor', [(0, 1), (1, 0)])  48.2 us
    ppermute x8, waiting for transfers between devices, flip(): return lax.ppermute(values, 'dp', [(i, i ^ 1 << bit) for i in range(size)])  36.7 us
    pallas_call x3, Pallas kernels, ffn(): pl.pallas_call(functools.partial(ffn_kernel, tiles), grid=(len(tiles),),...  32.6 us
    pallas_call x1, Pallas kernels, mixer_backward(): pl.pallas_call(functools.partial(backward_kernel, heads, len(grads)), gri...  28.2 us
    pallas_call x1, Pallas kernels, mixer_forward(): pl.pallas_call(functools.partial(forward_kernel, heads, subs), grid=(coun...  28.1 us
    all_gather x1, waiting for transfers between devices, local(): mix_full = lax.all_gather(mixer_pack, 'dp', axis=0, tiled=True)  25.8 us
    ppermute x13, starting transfers between devices, swap(): return lax.ppermute(rows, 'tensor', [(0, 1), (1, 0)])  17.5 us
    pallas_call x1, Pallas kernels, ffn_grads(): pl.pallas_call(functools.partial(ffn_grads_kernel, tiles), grid=(len(tile...  16.2 us
  transfers between devices with their start and end apart: 31, of which 10 were waited for; matrix products, arithmetic and copies ran while one was open for 15% of the time, Pallas kernels for 33%

profile of v1, /device:TPU:0, one launch (start us, length us, event | category | flops | bytes accessed | tf_op | source)
XLA Modules:
  0.0 363.8 jit_solution(12241850372811567131)
XLA Ops:
  15.0 2.9 collective-permute-start
  18.5 22.7 %collective-permute-done = bf16[512,1024]{1,0:T(8,128)(2,1)S(1)} collective-permute-done((bf16[512,1024]{1,0:T(8,128)(2,1)}, bf16[512,1024]{1,0:T(8,128)(2,1)S(1)}, u32[]{:S(2)}, u32[]{:S(2)}) %collective-permute-start) | collective-permute-done | bytes 1048608 | tf_op jit(solution)/shard_map/ppermute | solution.py:878
  46.1 25.8 %all-gather.3.cloned.1.call-done.weight_ref = bf16[1024,2688]{1,0:T(8,128)(2,1)} async-done(((bf16[64,2688]{1,0:T(8,128)(2,1)}), bf16[1024,2688]{1,0:T(8,128)(2,1)}) %all-gather.3.cloned.1.call-update) | async-done | bytes 5505040 | tf_op jit(solution)/shard_map/all_gather | solution.py:1032
  76.5 28.1 %mixer_forward.1 = (f32[1024,2176]{1,0:T(8,128)}, bf16[1024,512]{1,0:T(8,128)(2,1)}, bf16[1024,512]{1,0:T(8,128)(2,1)}, bf16[1024,512]{1,0:T(8,128)(2,1)}, bf16[...) custom-call(bf16[1024,1024]{1,0:T(8,128)(2,1)} %pad_maximum_fusion.x_ref.normed_r, ...), custom_call_target="tpu_custom_call" | custom-call | flops 26038239232 | bytes 28049408 | tf_op jit(solution)/shard_map/mixer_forward/pallas_call | solution.py:513
  107.0 13.2 %collective-permute-done.3 = bf16[512,512]{1,0:T(8,128)(2,1)S(1)} collective-permute-done((bf16[512,512]{1,0:T(8,128)(2,1)S(1)}, bf16[512,512]{1,0:T(8,128)(2,1)S(1)}, u32[]{:S(2)}, u32[]{:S(2)}) %collective-permute-start.3) | collective-permute-done | bytes 524320 | tf_op jit(solution)/shard_map/ppermute | solution.py:878
  121.0 2.1 multiply_reduce_fusion.2
  126.3 2.3 fusion.29
  128.6 10.7 %collective-permute-done.4.x_ref.refs_1_ = bf16[256,1024]{1,0:T(8,128)(2,1)} collective-permute-done((bf16[256,1024]{1,0:T(8,128)(2,1)S(1)}, bf16[256,1024]{1,0:T(8,128)(2,1)}, u32[]{:S(2)}, u32[]{:S(2)}) %collective-permute-start.4) | collective-permute-done | bytes 524320 | tf_op jit(solution)/shard_map/ppermute | solution.py:878
  139.3 10.7 %all-gather.5.cloned.1.call-done.w_ref = bf16[1024,4224]{1,0:T(8,128)(2,1)} async-done(((bf16[64,4224]{1,0:T(8,128)(2,1)}), bf16[1024,4224]{1,0:T(8,128)(2,1)}) %all-gather.5.cloned.1.call-update) | async-done | bytes 8650768 | tf_op jit(solution)/shard_map/all_gather | solution.py:1034
  150.0 8.9 %ffn.4 = (bf16[256,1408]{1,0:T(8,128)(2,1)}, bf16[256,2816]{1,0:T(8,128)(2,1)}, bf16[256,1024]{1,0:T(8,128)(2,1)}, bf16[256,1024]{1,0:T(8,128)(2,1)}) custom-call(bf16[256,1024]{1,0:T(8,128)(2,1)} %collective-permute-done.4.x_ref.refs_1_, bf16[256,1024]{1,0:T(8,128)(2,1)} %get-tuple-element.155.dy_ref.refs_4_, ...), custom_call_target="tpu_custom_call" | custom-call | flops 4429185024 | bytes 12910592 | tf_op jit(solution)/shard_map/ffn/pallas_call | solution.py:653
  160.4 9.1 %ffn.5 = (bf16[256,1408]{1,0:T(8,128)(2,1)}, bf16[256,2816]{1,0:T(8,128)(2,1)}, bf16[256,1024]{1,0:T(8,128)(2,1)}, bf16[256,1024]{1,0:T(8,128)(2,1)}) custom-call(bf16[256,1024]{1,0:T(8,128)(2,1)} %collective-permute-done.6.x_ref.refs_2_, bf16[256,1024]{1,0:T(8,128)(2,1)} %get-tuple-element.156.dy_ref.refs_5_, ...), custom_call_target="tpu_custom_call" | custom-call | flops 4429185024 | bytes 12910592 | tf_op jit(solution)/shard_map/ffn/pallas_call | solution.py:653
  170.1 14.6 %ffn.3 = (bf16[512,1408]{1,0:T(8,128)(2,1)}, bf16[512,2816]{1,0:T(8,128)(2,1)}, bf16[512,1024]{1,0:T(8,128)(2,1)}, bf16[512,1024]{1,0:T(8,128)(2,1)}) custom-call(bf16[512,1024]{1,0:T(8,128)(2,1)} %copy-done.3, bf16[512,1024]{1,0:T(8,128)(2,1)} %bitcast.75, bf16[1024,4224]{1,0:T(8,128)(2,1)} %all-gather.5.cloned.1.call-done.w_ref), custom_call_target="tpu_custom_call" | custom-call | flops 8858370048 | bytes 17170432 | tf_op jit(solution)/shard_map/ffn/pallas_call | solution.py:653
  192.0 16.2 %ffn_grads.1 = bf16[1024,4224]{1,0:T(8,128)(2,1)} custom-call(bf16[512,1024]{1,0:T(8,128)(2,1)} %copy-done.3, bf16[256,1024]{1,0:T(8,128)(2,1)} %collective-permute-done.4.x_ref.refs_1_, bf16[256,1024]{1,0:T(8,128)(2,1)} %collective-permute-done.6.x_ref.refs_2_, bf16[512,1024]{1,0:T(8,128)(2,1)} %bitcast.76, ...), custom_call_target="tpu_custom_call" | custom-call | flops 8858370048 | bytes 21495808 | tf_op jit(solution)/shard_map/ffn_grads/pallas_call | solution.py:722
  208.2 3.0 convolution_convert_fusion.1.refs_0_
  211.9 28.2 %mixer_backward.1 = (bf16[1024,2176]{1,0:T(8,128)(2,1)}, f32[12,512]{1,0:T(8,128)}, f32[1,128]{1,0:T(1,128)}, f32[1,128]{1,0:T(1,128)}) custom-call(s32[1]{0:T(128)} %bitcast.11.rank_ref, f32[1024,2176]{1,0:T(8,128)} %get-tuple-element.73.proj_ref.before_ref, f32[1024,128]{1,0:T(8,128)} %broadcast_in_dim.37.seg_ref.seg_before_ref, ...), custom_call_target="tpu_custom_call" | custom-call | flops 24159191040 | bytes 24117248 | tf_op jit(solution)/shard_map/mixer_backward/pallas_call | solution.py:588
  241.9 15.8 %mixer_grads.1 = (bf16[512,1280]{1,0:T(8,128)(2,1)}, bf16[512,1280]{1,0:T(8,128)(2,1)}, bf16[512,1408]{1,0:T(8,128)(2,1)}, bf16[512,1408]{1,0:T(8,128)(2,1)}) custom-call(s32[1]{0:T(128)} %bitcast.core_ref, bf16[1024,1024]{1,0:T(8,128)(2,1)} %pad_maximum_fusion.x_ref.normed_ref, bf16[1024,2176]{1,0:T(8,128)(2,1)} %get-tuple-element.105.dproj_ref, ...), custom_call_target="tpu_custom_call" | custom-call | flops 5637144576 | bytes 15204352 | tf_op jit(solution)/shard_map/mixer_grads/pallas_call | solution.py:823
  258.2 6.7 %fusion.15 = bf16[512,1024]{1,0:T(8,128)(2,1)} fusion(bf16[1024,2688]{1,0:T(8,128)(2,1)} %all-gather.3.cloned.1.call-done.weight_ref, bf16[1024,2176]{1,0:T(8,128)(2,1)} %get-tuple-element.105.dproj_ref, s32[]{:T(128)S(6)} %select_n.117), kind=kOutput, calls=%fused_computation.30 | convolution fusion | flops 2282225664 | bytes 7733252 | tf_op jit(solution)/shard_map/dot_general | solution.py:866
  265.0 2.2 add_convert_fusion.2
  267.3 2.1 add_convert_fusion.1
  272.9 25.1 %collective-permute-done.12 = bf16[256,1280]{1,0:T(8,128)(2,1)} collective-permute-done((bf16[256,1280]{1,0:T(8,128)(2,1)}, bf16[256,1280]{1,0:T(8,128)(2,1)}, u32[]{:S(2)}, u32[]{:S(2)}) %collective-permute-start.12) | collective-permute-done | bytes 655392 | tf_op jit(solution)/shard_map/ppermute | solution.py:975
  306.8 10.2 %collective-permute-done.13 = bf16[128,1280]{1,0:T(8,128)(2,1)S(1)} collective-permute-done((bf16[128,1280]{1,0:T(8,128)(2,1)S(1)}, bf16[128,1280]{1,0:T(8,128)(2,1)S(1)}, u32[]{:S(2)}, u32[]{:S(2)}) %collective-permute-start.13) | collective-permute-done | bytes 327712 | tf_op jit(solution)/shard_map/ppermute | solution.py:975
  318.9 5.2 %fusion.8 = (f32[1024]{0:T(1024)S(1)}, f32[512]{0:T(512)S(1)}, f32[512,1024]{1,0:T(8,128)S(1)}) fusion(bf16[1,512,1024]{2,1,0:T(8,128)(2,1)S(1)} %copy-done, f32[512]{0:T(512)S(1)} %fusion.23, bf16[512,1024]{1,0:T(8,128)(2,1)S(1)} %collective-permute-done.18, f32[1024]{0:T(1024)S(1)} %bitcast.90, bf16[512,2176]{1,0:T(8,128)(2,1)S(1)} %constant_dynamic-slice_fusion, ...), kind=kOutput, calls=%fused_computation.15 | convolution fusion | flops 2286418432 | bytes 10891264 | tf_op jit(solution)/shard_map/dot_general | solution.py:866
  325.5 2.4 collective-permute-done.19
  336.2 4.1 %collective-permute-start.25 = (f32[3,1024]{1,0:T(4,128)S(1)}, f32[3,1024]{1,0:T(4,128)S(1)}, u32[]{:S(2)}, u32[]{:S(2)}) collective-permute-start(f32[3,1024]{1,0:T(4,128)S(1)} %add_add_fusion.3), channel_id=1, source_target_pairs={{0,24},{2,26},{4,28},{6,30},{8,16},{10,18},{12,20},{14,22},{16,8},... | collective-permute-start | bytes 36872 | tf_op jit(solution)/shard_map/ppermute | solution.py:888
  (183 shorter events, 76.7 us)
Async XLA Ops:
  7.2 64.7 %all-gather.3.cloned.1.call-start = ((), (), s32[]{:S(2)}) async-start(), calls=%async_computation.1 | async-start | bytes 5849088 | tf_op jit(solution)/shard_map/all_gather | solution.py:1032
  11.7 138.3 %all-gather.5.cloned.1.call-start = ((), (), s32[]{:S(2)}) async-start(), calls=%async_computation.2 | async-start | bytes 9191424 | tf_op jit(solution)/shard_map/all_gather | solution.py:1034
  13.3 337.0 %reduce-scatter.2.cloned.1.call-start = ((), (), s32[]{:S(2)}) async-start(), calls=%async_computation.3 | async-start | bytes 9191424 | tf_op jit(solution)/shard_map/reduce_scatter | solution.py:1126
  15.0 26.3 %collective-permute-start = (bf16[512,1024]{1,0:T(8,128)(2,1)}, bf16[512,1024]{1,0:T(8,128)(2,1)S(1)}, u32[]{:S(2)}, u32[]{:S(2)}) collective-permute-start(bf16[512,1024]{1,0:T(8,128)(2,1)} %fusion.7), channel_id=1, source_target_pairs={{0,1},{1,0},{2,3},{3,2},{4,5},{5,4},{6,7},{7,6},{8,9},{9,8},{10,11... | collective-permute-start | bytes 3145736 | tf_op jit(solution)/shard_map/ppermute | solution.py:878
  42.3 30.9 %collective-permute-start.1 = (bf16[512,1024]{1,0:T(8,128)(2,1)S(1)}, bf16[512,1024]{1,0:T(8,128)(2,1)}, u32[]{:S(2)}, u32[]{:S(2)}) collective-permute-start(bf16[512,1024]{1,0:T(8,128)(2,1)S(1)} %bitcast.77), channel_id=1, source_target_pairs={{0,1},{1,0},{2,3},{3,2},{4,5},{5,4},{6,7},{7,6},{8,9},{9,8},{10,11... | collective-permute-start | bytes 3145736 | tf_op jit(solution)/shard_map/ppermute | solution.py:878
  75.1 29.6 %collective-permute-start.2 = (bf16[1024,512]{1,0:T(8,128)(2,1)S(1)}, bf16[1024,512]{1,0:T(8,128)(2,1)S(1)}, u32[]{:S(2)}, u32[]{:S(2)}) collective-permute-start(bf16[1024,512]{1,0:T(8,128)(2,1)S(1)} %slice.157), channel_id=1, source_target_pairs={{0,1},{1,0},{2,3},{3,2},{4,5},{5,4},{6,7},{7,6},{8,9},{9,8},{10,11... | collective-permute-start | bytes 3145736 | tf_op jit(solution)/shard_map/ppermute | solution.py:878
  106.3 13.9 %collective-permute-start.3 = (bf16[512,512]{1,0:T(8,128)(2,1)S(1)}, bf16[512,512]{1,0:T(8,128)(2,1)S(1)}, u32[]{:S(2)}, u32[]{:S(2)}) collective-permute-start(bf16[512,512]{1,0:T(8,128)(2,1)S(1)} %get-tuple-element.160.refs_3_), channel_id=1, source_target_pairs={{0,1},{1,0},{2,3},{3,2},{4,5},{5,4},{6,7},{7,6},{8,9},{9,8},{10,11... | collective-permute-start | bytes 1572872 | tf_op jit(solution)/shard_map/ppermute | solution.py:878
  124.3 15.0 %collective-permute-start.4 = (bf16[256,1024]{1,0:T(8,128)(2,1)S(1)}, bf16[256,1024]{1,0:T(8,128)(2,1)}, u32[]{:S(2)}, u32[]{:S(2)}) collective-permute-start(bf16[256,1024]{1,0:T(8,128)(2,1)S(1)} %get-tuple-element.157), channel_id=1, source_target_pairs={{0,1},{1,0},{2,3},{3,2},{4,5},{5,4},{6,7},{7,6},{8,9},{9,8},{10,11... | collective-permute-start | bytes 1572872 | tf_op jit(solution)/shard_map/ppermute | solution.py:878
  124.9 35.5 %collective-permute-start.6 = (bf16[256,1024]{1,0:T(8,128)(2,1)}, bf16[256,1024]{1,0:T(8,128)(2,1)}, u32[]{:S(2)}, u32[]{:S(2)}) collective-permute-start(bf16[256,1024]{1,0:T(8,128)(2,1)} %get-tuple-element.158), channel_id=1, source_target_pairs={{0,1},{1,0},{2,3},{3,2},{4,5},{5,4},{6,7},{7,6},{8,9},{9,8},{10,11... | collective-permute-start | bytes 1572872 | tf_op jit(solution)/shard_map/ppermute | solution.py:878
  158.8 25.9 %collective-permute-start.5 = (bf16[256,1024]{1,0:T(8,128)(2,1)}, bf16[256,1024]{1,0:T(8,128)(2,1)S(1)}, u32[]{:S(2)}, u32[]{:S(2)}) collective-permute-start(bf16[256,1024]{1,0:T(8,128)(2,1)} %get-tuple-element.80), channel_id=1, source_target_pairs={{0,1},{1,0},{2,3},{3,2},{4,5},{5,4},{6,7},{7,6},{8,9},{9,8},{10,11... | collective-permute-start | bytes 1572872 | tf_op jit(solution)/shard_map/ppermute | solution.py:878
  169.5 15.3 %collective-permute-start.7 = (bf16[256,1024]{1,0:T(8,128)(2,1)}, bf16[256,1024]{1,0:T(8,128)(2,1)S(1)}, u32[]{:S(2)}, u32[]{:S(2)}) collective-permute-start(bf16[256,1024]{1,0:T(8,128)(2,1)} %get-tuple-element.81), channel_id=1, source_target_pairs={{0,1},{1,0},{2,3},{3,2},{4,5},{5,4},{6,7},{7,6},{8,9},{9,8},{10,11... | collective-permute-start | bytes 1572872 | tf_op jit(solution)/shard_map/ppermute | solution.py:878
  190.5 20.7 %collective-permute-start.8 = (bf16[512,512]{1,0:T(8,128)(2,1)}, bf16[512,512]{1,0:T(8,128)(2,1)}, u32[]{:S(2)}, u32[]{:S(2)}) collective-permute-start(bf16[512,512]{1,0:T(8,128)(2,1)} %convolution_convert_fusion), channel_id=1, source_target_pairs={{0,1},{1,0},{2,3},{3,2},{4,5},{5,4},{6,7},{7,6},{8,9},{9,8},{10,11... | collective-permute-start | bytes 1572872 | tf_op jit(solution)/shard_map/ppermute | solution.py:878
  211.3 30.6 %collective-permute-start.9 = (bf16[512,1024]{1,0:T(8,128)(2,1)}, bf16[512,1024]{1,0:T(8,128)(2,1)}, u32[]{:S(2)}, u32[]{:S(2)}) collective-permute-start(bf16[512,1024]{1,0:T(8,128)(2,1)} %copy-done.14), channel_id=1, source_target_pairs={{0,1},{1,0},{2,3},{3,2},{4,5},{5,4},{6,7},{7,6},{8,9},{9,8},{10,11... | collective-permute-start | bytes 3145736 | tf_op jit(solution)/shard_map/ppermute | solution.py:878
  257.7 9.5 %collective-permute-start.11 = (bf16[512,1408]{1,0:T(8,128)(2,1)}, bf16[512,1408]{1,0:T(8,128)(2,1)}, u32[]{:S(2)}, u32[]{:S(2)}) collective-permute-start(bf16[512,1408]{1,0:T(8,128)(2,1)} %get-tuple-element.104), channel_id=1, source_target_pairs={{0,2},{2,0},{4,6},{6,4},{8,10},{10,8},{12,14},{14,12},{16,18},{18,... | collective-permute-start | bytes 4325384 | tf_op jit(solution)/shard_map/ppermute | solution.py:975
  269.4 28.6 %collective-permute-start.12 = (bf16[256,1280]{1,0:T(8,128)(2,1)}, bf16[256,1280]{1,0:T(8,128)(2,1)}, u32[]{:S(2)}, u32[]{:S(2)}) collective-permute-start(bf16[256,1280]{1,0:T(8,128)(2,1)} %add_convert_fusion.2), channel_id=1, source_target_pairs={{0,4},{2,6},{4,0},{6,2},{8,12},{10,14},{12,8},{14,10},{16,20},{18,... | collective-permute-start | bytes 1966088 | tf_op jit(solution)/shard_map/ppermute | solution.py:975
  270.0 32.1 %collective-permute-start.15 = (bf16[256,1408]{1,0:T(8,128)(2,1)}, bf16[256,1408]{1,0:T(8,128)(2,1)S(1)}, u32[]{:S(2)}, u32[]{:S(2)}) collective-permute-start(bf16[256,1408]{1,0:T(8,128)(2,1)} %add_convert_fusion.1), channel_id=1, source_target_pairs={{0,8},{2,10},{4,12},{6,14},{8,0},{10,2},{12,4},{14,6},{16,24},{18,... | collective-permute-start | bytes 2162696 | tf_op jit(solution)/shard_map/ppermute | solution.py:975
  271.3 47.6 %collective-permute-start.18 = (bf16[512,1024]{1,0:T(8,128)(2,1)}, bf16[512,1024]{1,0:T(8,128)(2,1)S(1)}, u32[]{:S(2)}, u32[]{:S(2)}) collective-permute-start(bf16[512,1024]{1,0:T(8,128)(2,1)} %fusion.15), channel_id=1, source_target_pairs={{0,1},{1,0},{2,3},{3,2},{4,5},{5,4},{6,7},{7,6},{8,9},{9,8},{10,11... | collective-permute-start | bytes 3145736 | tf_op jit(solution)/shard_map/ppermute | solution.py:878
  299.5 17.5 %collective-permute-start.13 = (bf16[128,1280]{1,0:T(8,128)(2,1)S(1)}, bf16[128,1280]{1,0:T(8,128)(2,1)S(1)}, u32[]{:S(2)}, u32[]{:S(2)}) collective-permute-start(bf16[128,1280]{1,0:T(8,128)(2,1)S(1)} %add_convert_fusion.4), channel_id=1, source_target_pairs={{0,8},{2,10},{4,12},{6,14},{8,0},{10,2},{12,4},{14,6},{16,24},{18,... | collective-permute-start | bytes 983048 | tf_op jit(solution)/shard_map/ppermute | solution.py:975
  303.3 32.8 %collective-permute-start.26 = (bf16[128,1408]{1,0:T(8,128)(2,1)S(1)}, bf16[128,1408]{1,0:T(8,128)(2,1)S(1)}, u32[]{:S(2)}, u32[]{:S(2)}) collective-permute-start(bf16[128,1408]{1,0:T(8,128)(2,1)S(1)} %add_convert_fusion.3), channel_id=1, source_target_pairs={{0,16},{2,18},{4,20},{6,22},{8,24},{10,26},{12,28},{14,30},{16,0},... | collective-permute-start | bytes 1081352 | tf_op jit(solution)/shard_map/ppermute | solution.py:975
  305.3 38.8 %collective-permute-start.16 = (bf16[256,1024]{1,0:T(8,128)(2,1)S(1)}, bf16[256,1024]{1,0:T(8,128)(2,1)S(1)}, u32[]{:S(2)}, u32[]{:S(2)}) collective-permute-start(bf16[256,1024]{1,0:T(8,128)(2,1)S(1)} %copy-done.21), channel_id=1, source_target_pairs={{0,1},{1,0},{2,3},{3,2},{4,5},{5,4},{6,7},{7,6},{8,9},{9,8},{10,11... | collective-permute-start | bytes 1572872 | tf_op jit(solution)/shard_map/ppermute | solution.py:878
  331.5 14.2 %collective-permute-start.17 = (bf16[256,1024]{1,0:T(8,128)(2,1)S(1)}, bf16[256,1024]{1,0:T(8,128)(2,1)S(1)}, u32[]{:S(2)}, u32[]{:S(2)}) collective-permute-start(bf16[256,1024]{1,0:T(8,128)(2,1)S(1)} %copy-done.22), channel_id=1, source_target_pairs={{0,1},{1,0},{2,3},{3,2},{4,5},{5,4},{6,7},{7,6},{8,9},{9,8},{10,11... | collective-permute-start | bytes 1572872 | tf_op jit(solution)/shard_map/ppermute | solution.py:878
  332.8 8.5 %collective-permute-start.23 = (f32[3,1024]{1,0:T(4,128)S(1)}, f32[3,1024]{1,0:T(4,128)S(1)}, u32[]{:S(2)}, u32[]{:S(2)}) collective-permute-start(f32[3,1024]{1,0:T(4,128)S(1)} %add_add_fusion.3), channel_id=1, source_target_pairs={{0,8},{2,10},{4,12},{6,14},{8,0},{10,2},{12,4},{14,6},{16,24},{18,... | collective-permute-start | bytes 36872 | tf_op jit(solution)/shard_map/ppermute | solution.py:888
  332.9 8.5 %collective-permute-start.24 = (f32[3,1024]{1,0:T(4,128)S(1)}, f32[3,1024]{1,0:T(4,128)S(1)}, u32[]{:S(2)}, u32[]{:S(2)}) collective-permute-start(f32[3,1024]{1,0:T(4,128)S(1)} %add_add_fusion.3), channel_id=1, source_target_pairs={{0,16},{2,18},{4,20},{6,22},{8,24},{10,26},{12,28},{14,30},{16,0},... | collective-permute-start | bytes 36872 | tf_op jit(solution)/shard_map/ppermute | solution.py:888
  341.4 11.8 %collective-permute-start.14 = (bf16[64,1280]{1,0:T(8,128)(2,1)}, bf16[64,1280]{1,0:T(8,128)(2,1)}, u32[]{:S(2)}, u32[]{:S(2)}) collective-permute-start(bf16[64,1280]{1,0:T(8,128)(2,1)} %add_convert_fusion.6), channel_id=1, source_target_pairs={{0,16},{2,18},{4,20},{6,22},{8,24},{10,26},{12,28},{14,30},{16,0},... | collective-permute-start | bytes 491528 | tf_op jit(solution)/shard_map/ppermute | solution.py:975
  (32 other events, 207.9 us)
Sparse Core Ops, SparseCore 0:
  11.8 60.0 all-gather.2
  74.8 75.1 all-gather.4
  211.4 130.0 reduce-scatter.1

commit v2 on v1

--- a/solution.py
+++ b/solution.py
@@ -1142,9 +1142,10 @@
     first_out = outgoing(first, bits[0][1])
     if pair:
         grad_here, grad_there = own_and_other(projection_grad)
-        sent = contract_last(grad_there, mix_rows).astype(bf16)
-        first_out, second_out, sent = lax.optimization_barrier((first_out, second_out, sent))
-        received = swap(sent)
+        first_out, second_out, grad_there = lax.optimization_barrier(
+            (first_out, second_out, grad_there)
+        )
+        received = swap(contract_last(grad_there, mix_rows).astype(bf16))
     else:
         received = scatter_rows(contract_last(projection_grad, mix_rows))
     first = settle(first, bits[0][1], first_out)

time: 368 us -> 366 us (level)
  waiting for transfers between devices: 124 us -> 113 us
    ppermute x8, waiting for transfers between devices: 36.7 us -> 26.4 us  [flip(): return lax.ppermute(values, 'dp', [(i, i ^ 1 << bit) for i in range(size)])]
  transfers between devices with their start and end apart: 31 -> 31, of which waited for: 10 -> 10; matrix products, arithmetic and copies ran while one was open for 15% -> 17% of each run, Pallas kernels for 33% -> 34%
where the time goes in v2:
time: 366 us; the launch traced here: 361 us
  Pallas kernels  121 us (33%)
  waiting for transfers between devices  113 us (31%)
  starting transfers between devices  36.5 us (10%)
  local copies, waits for them, and re-layouts  29.9 us (8%)
  other arithmetic  26.8 us (7%)
  matrix products  19 us (5%)
  between operations  14.6 us (4%)
    ppermute x13, waiting for transfers between devices, swap(): return lax.ppermute(rows, 'tensor', [(0, 1), (1, 0)])  46.7 us
    pallas_call x3, Pallas kernels, ffn(): pl.pallas_call(functools.partial(ffn_kernel, tiles), grid=(len(tiles),),...  32.5 us
    pallas_call x1, Pallas kernels, mixer_backward(): pl.pallas_call(functools.partial(backward_kernel, heads, len(grads)), gri...  28.2 us
    pallas_call x1, Pallas kernels, mixer_forward(): pl.pallas_call(functools.partial(forward_kernel, heads, subs), grid=(coun...  28.1 us
    ppermute x8, waiting for transfers between devices, flip(): return lax.ppermute(values, 'dp', [(i, i ^ 1 << bit) for i in range(size)])  26.4 us
    all_gather x1, waiting for transfers between devices, local(): mix_full = lax.all_gather(mixer_pack, 'dp', axis=0, tiled=True)  25.8 us
    ppermute x13, starting transfers between devices, swap(): return lax.ppermute(rows, 'tensor', [(0, 1), (1, 0)])  17.3 us
    pallas_call x1, Pallas kernels, ffn_grads(): pl.pallas_call(functools.partial(ffn_grads_kernel, tiles), grid=(len(tile...  16.2 us
  transfers between devices with their start and end apart: 31, of which 10 were waited for; matrix products, arithmetic and copies ran while one was open for 17% of the time, Pallas kernels for 34%

profile of v2, /device:TPU:0, one launch (start us, length us, event | category | flops | bytes accessed | tf_op | source)
XLA Modules:
  0.0 360.6 jit_solution(13461831809840370650)
XLA Ops:
  15.0 2.9 collective-permute-start
  18.5 22.7 %collective-permute-done = bf16[512,1024]{1,0:T(8,128)(2,1)S(1)} collective-permute-done((bf16[512,1024]{1,0:T(8,128)(2,1)}, bf16[512,1024]{1,0:T(8,128)(2,1)S(1)}, u32[]{:S(2)}, u32[]{:S(2)}) %collective-permute-start) | collective-permute-done | bytes 1048608 | tf_op jit(solution)/shard_map/ppermute | solution.py:878
  46.1 25.8 %all-gather.3.cloned.1.call-done.weight_ref = bf16[1024,2688]{1,0:T(8,128)(2,1)} async-done(((bf16[64,2688]{1,0:T(8,128)(2,1)}), bf16[1024,2688]{1,0:T(8,128)(2,1)}) %all-gather.3.cloned.1.call-update) | async-done | bytes 5505040 | tf_op jit(solution)/shard_map/all_gather | solution.py:1032
  76.5 28.1 %mixer_forward.1 = (f32[1024,2176]{1,0:T(8,128)}, bf16[1024,512]{1,0:T(8,128)(2,1)}, bf16[1024,512]{1,0:T(8,128)(2,1)}, bf16[1024,512]{1,0:T(8,128)(2,1)}, bf16[...) custom-call(bf16[1024,1024]{1,0:T(8,128)(2,1)} %pad_maximum_fusion.x_ref.normed_r, ...), custom_call_target="tpu_custom_call" | custom-call | flops 26038239232 | bytes 28049408 | tf_op jit(solution)/shard_map/mixer_forward/pallas_call | solution.py:513
  107.0 13.2 %collective-permute-done.3 = bf16[512,512]{1,0:T(8,128)(2,1)S(1)} collective-permute-done((bf16[512,512]{1,0:T(8,128)(2,1)S(1)}, bf16[512,512]{1,0:T(8,128)(2,1)S(1)}, u32[]{:S(2)}, u32[]{:S(2)}) %collective-permute-start.3) | collective-permute-done | bytes 524320 | tf_op jit(solution)/shard_map/ppermute | solution.py:878
  126.4 2.3 fusion.25
  128.6 10.7 %collective-permute-done.4.x_ref.refs_1_ = bf16[256,1024]{1,0:T(8,128)(2,1)} collective-permute-done((bf16[256,1024]{1,0:T(8,128)(2,1)S(1)}, bf16[256,1024]{1,0:T(8,128)(2,1)}, u32[]{:S(2)}, u32[]{:S(2)}) %collective-permute-start.4) | collective-permute-done | bytes 524320 | tf_op jit(solution)/shard_map/ppermute | solution.py:878
  139.3 10.6 %all-gather.5.cloned.1.call-done.w_ref = bf16[1024,4224]{1,0:T(8,128)(2,1)} async-done(((bf16[64,4224]{1,0:T(8,128)(2,1)}), bf16[1024,4224]{1,0:T(8,128)(2,1)}) %all-gather.5.cloned.1.call-update) | async-done | bytes 8650768 | tf_op jit(solution)/shard_map/all_gather | solution.py:1034
  150.0 8.9 %ffn.4 = (bf16[256,1408]{1,0:T(8,128)(2,1)}, bf16[256,2816]{1,0:T(8,128)(2,1)}, bf16[256,1024]{1,0:T(8,128)(2,1)}, bf16[256,1024]{1,0:T(8,128)(2,1)}) custom-call(bf16[256,1024]{1,0:T(8,128)(2,1)} %collective-permute-done.4.x_ref.refs_1_, bf16[256,1024]{1,0:T(8,128)(2,1)} %get-tuple-element.157.dy_ref.refs_4_, ...), custom_call_target="tpu_custom_call" | custom-call | flops 4429185024 | bytes 12910592 | tf_op jit(solution)/shard_map/ffn/pallas_call | solution.py:653
  160.4 9.1 %ffn.5 = (bf16[256,1408]{1,0:T(8,128)(2,1)}, bf16[256,2816]{1,0:T(8,128)(2,1)}, bf16[256,1024]{1,0:T(8,128)(2,1)}, bf16[256,1024]{1,0:T(8,128)(2,1)}) custom-call(bf16[256,1024]{1,0:T(8,128)(2,1)} %collective-permute-done.6.x_ref.refs_2_, bf16[256,1024]{1,0:T(8,128)(2,1)} %get-tuple-element.158.dy_ref.refs_5_, ...), custom_call_target="tpu_custom_call" | custom-call | flops 4429185024 | bytes 12910592 | tf_op jit(solution)/shard_map/ffn/pallas_call | solution.py:653
  170.1 14.6 %ffn.3 = (bf16[512,1408]{1,0:T(8,128)(2,1)}, bf16[512,2816]{1,0:T(8,128)(2,1)}, bf16[512,1024]{1,0:T(8,128)(2,1)}, bf16[512,1024]{1,0:T(8,128)(2,1)}) custom-call(bf16[512,1024]{1,0:T(8,128)(2,1)} %copy-done.3, bf16[512,1024]{1,0:T(8,128)(2,1)} %bitcast.76, bf16[1024,4224]{1,0:T(8,128)(2,1)} %all-gather.5.cloned.1.call-done.w_ref), custom_call_target="tpu_custom_call" | custom-call | flops 8858370048 | bytes 17170432 | tf_op jit(solution)/shard_map/ffn/pallas_call | solution.py:653
  191.9 16.2 %ffn_grads.1 = bf16[1024,4224]{1,0:T(8,128)(2,1)} custom-call(bf16[512,1024]{1,0:T(8,128)(2,1)} %copy-done.3, bf16[256,1024]{1,0:T(8,128)(2,1)} %collective-permute-done.4.x_ref.refs_1_, bf16[256,1024]{1,0:T(8,128)(2,1)} %collective-permute-done.6.x_ref.refs_2_, bf16[512,1024]{1,0:T(8,128)(2,1)} %bitcast.77, ...), custom_call_target="tpu_custom_call" | custom-call | flops 8858370048 | bytes 21495808 | tf_op jit(solution)/shard_map/ffn_grads/pallas_call | solution.py:722
  208.1 3.0 convolution_convert_fusion.1.refs_0_
  211.8 28.2 %mixer_backward.1 = (bf16[1024,2176]{1,0:T(8,128)(2,1)}, f32[12,512]{1,0:T(8,128)}, f32[1,128]{1,0:T(1,128)}, f32[1,128]{1,0:T(1,128)}) custom-call(s32[1]{0:T(128)} %bitcast.11.rank_ref, f32[1024,2176]{1,0:T(8,128)} %get-tuple-element.73.proj_ref.before_ref, f32[1024,128]{1,0:T(8,128)} %broadcast_in_dim.37.seg_ref.seg_before_ref, ...), custom_call_target="tpu_custom_call" | custom-call | flops 24159191040 | bytes 24117248 | tf_op jit(solution)/shard_map/mixer_backward/pallas_call | solution.py:588
  241.8 15.8 %mixer_grads.1 = (bf16[512,1280]{1,0:T(8,128)(2,1)}, bf16[512,1280]{1,0:T(8,128)(2,1)}, bf16[512,1408]{1,0:T(8,128)(2,1)}, bf16[512,1408]{1,0:T(8,128)(2,1)}) custom-call(s32[1]{0:T(128)} %bitcast.core_ref, bf16[1024,1024]{1,0:T(8,128)(2,1)} %pad_maximum_fusion.x_ref.normed_ref, bf16[1024,2176]{1,0:T(8,128)(2,1)} %get-tuple-element.105.dproj_ref, ...), custom_call_target="tpu_custom_call" | custom-call | flops 5637144576 | bytes 15204352 | tf_op jit(solution)/shard_map/mixer_grads/pallas_call | solution.py:823
  258.2 4.2 %constant_dynamic-slice_fusion = (bf16[512,2176]{1,0:T(8,128)(2,1)}, bf16[512,2176]{1,0:T(8,128)(2,1)S(1)}) fusion(bf16[1024,2176]{1,0:T(8,128)(2,1)} %get-tuple-element.105.dproj_ref, s32[]{:T(128)S(6)} %select_n.116, s32[]{:T(128)S(6)} %select_n.117), kind=kLoop, calls=%fused_computation.68 | loop fusion | bytes 8912904 | tf_op jit(solution)/shard_map/dynamic_slice | solution.py:1016
  262.4 2.2 add_convert_fusion.2
  268.6 5.9 %fusion.14 = bf16[512,1024]{1,0:T(8,128)(2,1)} fusion(bf16[512,2176]{1,0:T(8,128)(2,1)S(1)} %get-tuple-element.115, bf16[1024,2688]{1,0:T(8,128)(2,1)} %all-gather.3.cloned.1.call-done.weight_ref), kind=kOutput, calls=%fused_computation.29 | convolution fusion | flops 2282225664 | bytes 7733248 | tf_op jit(solution)/shard_map/dot_general | solution.py:866
  276.3 19.6 %collective-permute-done.12 = bf16[256,1280]{1,0:T(8,128)(2,1)} collective-permute-done((bf16[256,1280]{1,0:T(8,128)(2,1)}, bf16[256,1280]{1,0:T(8,128)(2,1)}, u32[]{:S(2)}, u32[]{:S(2)}) %collective-permute-start.12) | collective-permute-done | bytes 655392 | tf_op jit(solution)/shard_map/ppermute | solution.py:975
  303.1 6.5 %collective-permute-done.13 = bf16[128,1280]{1,0:T(8,128)(2,1)S(1)} collective-permute-done((bf16[128,1280]{1,0:T(8,128)(2,1)S(1)}, bf16[128,1280]{1,0:T(8,128)(2,1)S(1)}, u32[]{:S(2)}, u32[]{:S(2)}) %collective-permute-start.13) | collective-permute-done | bytes 327712 | tf_op jit(solution)/shard_map/ppermute | solution.py:975
  311.5 5.8 %fusion.7 = (f32[1024]{0:T(1024)S(1)}, f32[512]{0:T(512)S(1)}, f32[512,1024]{1,0:T(8,128)S(1)}) fusion(bf16[1,512,1024]{2,1,0:T(8,128)(2,1)S(1)} %copy-done, f32[512]{0:T(512)S(1)} %fusion.19, bf16[512,1024]{1,0:T(8,128)(2,1)} %collective-permute-done.18, f32[1024]{0:T(1024)S(1)} %bitcast.91, bf16[512,2176]{1,0:T(8,128)(2,1)S(1)} %copy-done.4, ...), kind=kOutput, calls=%fused_computation.14 | convolution fusion | flops 2286418432 | bytes 10891264 | tf_op jit(solution)/shard_map/dot_general | solution.py:866
  318.8 2.4 collective-permute-done.19
  323.0 3.0 fusion.18
  328.0 6.6 %collective-permute-start.24 = (f32[3,1024]{1,0:T(4,128)S(1)}, f32[3,1024]{1,0:T(4,128)S(1)}, u32[]{:S(2)}, u32[]{:S(2)}) collective-permute-start(f32[3,1024]{1,0:T(4,128)S(1)} %add_add_fusion.3), channel_id=1, source_target_pairs={{0,16},{2,18},{4,20},{6,22},{8,24},{10,26},{12,28},{14,30},{16,0},... | collective-permute-start | bytes 36872 | tf_op jit(solution)/shard_map/ppermute | solution.py:888
  (183 shorter events, 77.7 us)
Async XLA Ops:
  7.2 64.7 %all-gather.3.cloned.1.call-start = ((), (), s32[]{:S(2)}) async-start(), calls=%async_computation.1 | async-start | bytes 5849088 | tf_op jit(solution)/shard_map/all_gather | solution.py:1032
  11.7 138.3 %all-gather.5.cloned.1.call-start = ((), (), s32[]{:S(2)}) async-start(), calls=%async_computation.2 | async-start | bytes 9191424 | tf_op jit(solution)/shard_map/all_gather | solution.py:1034
  13.3 333.8 %reduce-scatter.2.cloned.1.call-start = ((), (), s32[]{:S(2)}) async-start(), calls=%async_computation.3 | async-start | bytes 9191424 | tf_op jit(solution)/shard_map/reduce_scatter | solution.py:1126
  15.0 26.3 %collective-permute-start = (bf16[512,1024]{1,0:T(8,128)(2,1)}, bf16[512,1024]{1,0:T(8,128)(2,1)S(1)}, u32[]{:S(2)}, u32[]{:S(2)}) collective-permute-start(bf16[512,1024]{1,0:T(8,128)(2,1)} %fusion.6), channel_id=1, source_target_pairs={{0,1},{1,0},{2,3},{3,2},{4,5},{5,4},{6,7},{7,6},{8,9},{9,8},{10,11... | collective-permute-start | bytes 3145736 | tf_op jit(solution)/shard_map/ppermute | solution.py:878
  42.3 30.9 %collective-permute-start.1 = (bf16[512,1024]{1,0:T(8,128)(2,1)S(1)}, bf16[512,1024]{1,0:T(8,128)(2,1)}, u32[]{:S(2)}, u32[]{:S(2)}) collective-permute-start(bf16[512,1024]{1,0:T(8,128)(2,1)S(1)} %bitcast.78), channel_id=1, source_target_pairs={{0,1},{1,0},{2,3},{3,2},{4,5},{5,4},{6,7},{7,6},{8,9},{9,8},{10,11... | collective-permute-start | bytes 3145736 | tf_op jit(solution)/shard_map/ppermute | solution.py:878
  75.1 29.6 %collective-permute-start.2 = (bf16[1024,512]{1,0:T(8,128)(2,1)S(1)}, bf16[1024,512]{1,0:T(8,128)(2,1)S(1)}, u32[]{:S(2)}, u32[]{:S(2)}) collective-permute-start(bf16[1024,512]{1,0:T(8,128)(2,1)S(1)} %slice.157), channel_id=1, source_target_pairs={{0,1},{1,0},{2,3},{3,2},{4,5},{5,4},{6,7},{7,6},{8,9},{9,8},{10,11... | collective-permute-start | bytes 3145736 | tf_op jit(solution)/shard_map/ppermute | solution.py:878
  106.3 13.9 %collective-permute-start.3 = (bf16[512,512]{1,0:T(8,128)(2,1)S(1)}, bf16[512,512]{1,0:T(8,128)(2,1)S(1)}, u32[]{:S(2)}, u32[]{:S(2)}) collective-permute-start(bf16[512,512]{1,0:T(8,128)(2,1)S(1)} %get-tuple-element.162.refs_3_), channel_id=1, source_target_pairs={{0,1},{1,0},{2,3},{3,2},{4,5},{5,4},{6,7},{7,6},{8,9},{9,8},{10,11... | collective-permute-start | bytes 1572872 | tf_op jit(solution)/shard_map/ppermute | solution.py:878
  124.3 15.0 %collective-permute-start.4 = (bf16[256,1024]{1,0:T(8,128)(2,1)S(1)}, bf16[256,1024]{1,0:T(8,128)(2,1)}, u32[]{:S(2)}, u32[]{:S(2)}) collective-permute-start(bf16[256,1024]{1,0:T(8,128)(2,1)S(1)} %get-tuple-element.159), channel_id=1, source_target_pairs={{0,1},{1,0},{2,3},{3,2},{4,5},{5,4},{6,7},{7,6},{8,9},{9,8},{10,11... | collective-permute-start | bytes 1572872 | tf_op jit(solution)/shard_map/ppermute | solution.py:878
  124.9 35.4 %collective-permute-start.6 = (bf16[256,1024]{1,0:T(8,128)(2,1)}, bf16[256,1024]{1,0:T(8,128)(2,1)}, u32[]{:S(2)}, u32[]{:S(2)}) collective-permute-start(bf16[256,1024]{1,0:T(8,128)(2,1)} %get-tuple-element.160), channel_id=1, source_target_pairs={{0,1},{1,0},{2,3},{3,2},{4,5},{5,4},{6,7},{7,6},{8,9},{9,8},{10,11... | collective-permute-start | bytes 1572872 | tf_op jit(solution)/shard_map/ppermute | solution.py:878
  158.8 25.9 %collective-permute-start.5 = (bf16[256,1024]{1,0:T(8,128)(2,1)}, bf16[256,1024]{1,0:T(8,128)(2,1)S(1)}, u32[]{:S(2)}, u32[]{:S(2)}) collective-permute-start(bf16[256,1024]{1,0:T(8,128)(2,1)} %get-tuple-element.80), channel_id=1, source_target_pairs={{0,1},{1,0},{2,3},{3,2},{4,5},{5,4},{6,7},{7,6},{8,9},{9,8},{10,11... | collective-permute-start | bytes 1572872 | tf_op jit(solution)/shard_map/ppermute | solution.py:878
  169.5 15.2 %collective-permute-start.7 = (bf16[256,1024]{1,0:T(8,128)(2,1)}, bf16[256,1024]{1,0:T(8,128)(2,1)S(1)}, u32[]{:S(2)}, u32[]{:S(2)}) collective-permute-start(bf16[256,1024]{1,0:T(8,128)(2,1)} %get-tuple-element.81), channel_id=1, source_target_pairs={{0,1},{1,0},{2,3},{3,2},{4,5},{5,4},{6,7},{7,6},{8,9},{9,8},{10,11... | collective-permute-start | bytes 1572872 | tf_op jit(solution)/shard_map/ppermute | solution.py:878
  190.4 20.7 %collective-permute-start.8 = (bf16[512,512]{1,0:T(8,128)(2,1)}, bf16[512,512]{1,0:T(8,128)(2,1)}, u32[]{:S(2)}, u32[]{:S(2)}) collective-permute-start(bf16[512,512]{1,0:T(8,128)(2,1)} %convolution_convert_fusion), channel_id=1, source_target_pairs={{0,1},{1,0},{2,3},{3,2},{4,5},{5,4},{6,7},{7,6},{8,9},{9,8},{10,11... | collective-permute-start | bytes 1572872 | tf_op jit(solution)/shard_map/ppermute | solution.py:878
  211.2 30.6 %collective-permute-start.9 = (bf16[512,1024]{1,0:T(8,128)(2,1)}, bf16[512,1024]{1,0:T(8,128)(2,1)}, u32[]{:S(2)}, u32[]{:S(2)}) collective-permute-start(bf16[512,1024]{1,0:T(8,128)(2,1)} %copy-done.14), channel_id=1, source_target_pairs={{0,1},{1,0},{2,3},{3,2},{4,5},{5,4},{6,7},{7,6},{8,9},{9,8},{10,11... | collective-permute-start | bytes 3145736 | tf_op jit(solution)/shard_map/ppermute | solution.py:878
  257.7 6.9 %collective-permute-start.11 = (bf16[512,1408]{1,0:T(8,128)(2,1)}, bf16[512,1408]{1,0:T(8,128)(2,1)}, u32[]{:S(2)}, u32[]{:S(2)}) collective-permute-start(bf16[512,1408]{1,0:T(8,128)(2,1)} %get-tuple-element.104), channel_id=1, source_target_pairs={{0,2},{2,0},{4,6},{6,4},{8,10},{10,8},{12,14},{14,12},{16,18},{18,... | collective-permute-start | bytes 4325384 | tf_op jit(solution)/shard_map/ppermute | solution.py:975
  266.8 31.9 %collective-permute-start.15 = (bf16[256,1408]{1,0:T(8,128)(2,1)}, bf16[256,1408]{1,0:T(8,128)(2,1)}, u32[]{:S(2)}, u32[]{:S(2)}) collective-permute-start(bf16[256,1408]{1,0:T(8,128)(2,1)} %add_convert_fusion.1), channel_id=1, source_target_pairs={{0,8},{2,10},{4,12},{6,14},{8,0},{10,2},{12,4},{14,6},{16,24},{18,... | collective-permute-start | bytes 2162696 | tf_op jit(solution)/shard_map/ppermute | solution.py:975
  267.6 28.3 %collective-permute-start.12 = (bf16[256,1280]{1,0:T(8,128)(2,1)}, bf16[256,1280]{1,0:T(8,128)(2,1)}, u32[]{:S(2)}, u32[]{:S(2)}) collective-permute-start(bf16[256,1280]{1,0:T(8,128)(2,1)} %add_convert_fusion.2), channel_id=1, source_target_pairs={{0,4},{2,6},{4,0},{6,2},{8,12},{10,14},{12,8},{14,10},{16,20},{18,... | collective-permute-start | bytes 1966088 | tf_op jit(solution)/shard_map/ppermute | solution.py:975
  274.5 37.1 %collective-permute-start.18 = (bf16[512,1024]{1,0:T(8,128)(2,1)}, bf16[512,1024]{1,0:T(8,128)(2,1)}, u32[]{:S(2)}, u32[]{:S(2)}) collective-permute-start(bf16[512,1024]{1,0:T(8,128)(2,1)} %fusion.14), channel_id=1, source_target_pairs={{0,1},{1,0},{2,3},{3,2},{4,5},{5,4},{6,7},{7,6},{8,9},{9,8},{10,11... | collective-permute-start | bytes 3145736 | tf_op jit(solution)/shard_map/ppermute | solution.py:878
  297.3 12.3 %collective-permute-start.13 = (bf16[128,1280]{1,0:T(8,128)(2,1)S(1)}, bf16[128,1280]{1,0:T(8,128)(2,1)S(1)}, u32[]{:S(2)}, u32[]{:S(2)}) collective-permute-start(bf16[128,1280]{1,0:T(8,128)(2,1)S(1)} %add_convert_fusion.4), channel_id=1, source_target_pairs={{0,8},{2,10},{4,12},{6,14},{8,0},{10,2},{12,4},{14,6},{16,24},{18,... | collective-permute-start | bytes 983048 | tf_op jit(solution)/shard_map/ppermute | solution.py:975
  300.1 34.5 %collective-permute-start.26 = (bf16[128,1408]{1,0:T(8,128)(2,1)S(1)}, bf16[128,1408]{1,0:T(8,128)(2,1)S(1)}, u32[]{:S(2)}, u32[]{:S(2)}) collective-permute-start(bf16[128,1408]{1,0:T(8,128)(2,1)S(1)} %add_convert_fusion.3), channel_id=1, source_target_pairs={{0,16},{2,18},{4,20},{6,22},{8,24},{10,26},{12,28},{14,30},{16,0},... | collective-permute-start | bytes 1081352 | tf_op jit(solution)/shard_map/ppermute | solution.py:975
  301.7 40.3 %collective-permute-start.16 = (bf16[256,1024]{1,0:T(8,128)(2,1)S(1)}, bf16[256,1024]{1,0:T(8,128)(2,1)S(1)}, u32[]{:S(2)}, u32[]{:S(2)}) collective-permute-start(bf16[256,1024]{1,0:T(8,128)(2,1)S(1)} %copy-done.21), channel_id=1, source_target_pairs={{0,1},{1,0},{2,3},{3,2},{4,5},{5,4},{6,7},{7,6},{8,9},{9,8},{10,11... | collective-permute-start | bytes 1572872 | tf_op jit(solution)/shard_map/ppermute | solution.py:878
  326.0 15.9 %collective-permute-start.17 = (bf16[256,1024]{1,0:T(8,128)(2,1)S(1)}, bf16[256,1024]{1,0:T(8,128)(2,1)S(1)}, u32[]{:S(2)}, u32[]{:S(2)}) collective-permute-start(bf16[256,1024]{1,0:T(8,128)(2,1)S(1)} %copy-done.22), channel_id=1, source_target_pairs={{0,1},{1,0},{2,3},{3,2},{4,5},{5,4},{6,7},{7,6},{8,9},{9,8},{10,11... | collective-permute-start | bytes 1572872 | tf_op jit(solution)/shard_map/ppermute | solution.py:878
  327.4 8.5 %collective-permute-start.23 = (f32[3,1024]{1,0:T(4,128)S(1)}, f32[3,1024]{1,0:T(4,128)S(1)}, u32[]{:S(2)}, u32[]{:S(2)}) collective-permute-start(f32[3,1024]{1,0:T(4,128)S(1)} %add_add_fusion.3), channel_id=1, source_target_pairs={{0,8},{2,10},{4,12},{6,14},{8,0},{10,2},{12,4},{14,6},{16,24},{18,... | collective-permute-start | bytes 36872 | tf_op jit(solution)/shard_map/ppermute | solution.py:888
  328.0 9.5 %collective-permute-start.24 = (f32[3,1024]{1,0:T(4,128)S(1)}, f32[3,1024]{1,0:T(4,128)S(1)}, u32[]{:S(2)}, u32[]{:S(2)}) collective-permute-start(f32[3,1024]{1,0:T(4,128)S(1)} %add_add_fusion.3), channel_id=1, source_target_pairs={{0,16},{2,18},{4,20},{6,22},{8,24},{10,26},{12,28},{14,30},{16,0},... | collective-permute-start | bytes 36872 | tf_op jit(solution)/shard_map/ppermute | solution.py:888
  336.0 14.0 %collective-permute-start.14 = (bf16[64,1280]{1,0:T(8,128)(2,1)}, bf16[64,1280]{1,0:T(8,128)(2,1)}, u32[]{:S(2)}, u32[]{:S(2)}) collective-permute-start(bf16[64,1280]{1,0:T(8,128)(2,1)} %add_convert_fusion.6), channel_id=1, source_target_pairs={{0,16},{2,18},{4,20},{6,22},{8,24},{10,26},{12,28},{14,30},{16,0},... | collective-permute-start | bytes 491528 | tf_op jit(solution)/shard_map/ppermute | solution.py:975
  (32 other events, 293.7 us)
Sparse Core Ops, SparseCore 0:
  11.8 60.0 all-gather.2
  74.8 75.1 all-gather.4
  211.3 124.4 reduce-scatter.1
